TPU v7x, 32 devices: a whole 2x2x4 slice. The times are simulated.
32 devices in a mesh: group: 4 (over x, core), fsdp: 8 (over z, y).
Axes of the slice: x: 2, y: 2, z: 4, core: 2. Of those that a mesh axis runs over, the one named last changes fastest.
Arguments:
- inputs: bfloat16 [4, 8192, 768], P('group', 'fsdp'), may hold values from -6 to 6
- segments: int32 [4, 128, 64], P('group', 'fsdp'), may hold values from 0 to 7, never falling along the last dimension, each value on 1 to 32 neighbouring positions
- cotangent: bfloat16 [4, 8192, 768], P('group', 'fsdp'), may hold values from -6 to 6
- attn_weight: float32 [768, 3072], P('fsdp'), may hold values from -0.5412659 to 0.5412659
- attn_first: float32 [4, 768, 3072], P('group', 'fsdp'), may hold values from -64 to 64
- attn_second: float32 [4, 768, 3072], P('group', 'fsdp'), may hold values from 8.192 to 32.768
- attn_outer: float32 [768, 3072], P('fsdp'), may hold values from -0.125 to 0.125
- mlp_weight: float32 [2, 768, 3072], P(None, 'fsdp'), may hold values from -0.21875 to 0.21875
- mlp_first: float32 [4, 2, 768, 3072], P('group', None, 'fsdp'), may hold values from -64 to 64
- mlp_second: float32 [4, 2, 768, 3072], P('group', None, 'fsdp'), may hold values from 8.192 to 32.768
- mlp_outer: float32 [2, 768, 3072], P(None, 'fsdp'), may hold values from -0.125 to 0.125
- vector_weight: float32 [12, 768], P(None, 'fsdp'), may hold values from -0.9 to 1.75
- vector_first: float32 [4, 12, 768], P('group', None, 'fsdp'), may hold values from -64 to 64
- vector_second: float32 [4, 12, 768], P('group', None, 'fsdp'), may hold values from 8.192 to 32.768
- vector_outer: float32 [12, 768], P(None, 'fsdp'), may hold values from -1.25 to 1.25
Outputs:
- block_out: bfloat16 [4, 8192, 768], P('group', 'fsdp')
- input_grad: float32 [4, 8192, 768], P('group', 'fsdp')
- attn_moment: float32 [4, 768, 3072], P('group', 'fsdp')
- attn_square: float32 [4, 768, 3072], P('group', 'fsdp')
- attn_momentum: float32 [768, 3072], P('fsdp')
- attn_master: float32 [768, 3072], P('fsdp')
- mlp_moment: float32 [4, 2, 768, 3072], P('group', None, 'fsdp')
- mlp_square: float32 [4, 2, 768, 3072], P('group', None, 'fsdp')
- mlp_momentum: float32 [2, 768, 3072], P(None, 'fsdp')
- mlp_master: float32 [2, 768, 3072], P(None, 'fsdp')
- vector_moment: float32 [4, 12, 768], P('group', None, 'fsdp')
- vector_square: float32 [4, 12, 768], P('group', None, 'fsdp')
- vector_momentum: float32 [12, 768], P(None, 'fsdp')
- vector_master: float32 [12, 768], P(None, 'fsdp')
Inputs may be any that keep to these rules, and one draw needn't show every extreme that they name: `segments`: segments of a packed row are numbered from 0 upwards, never falling; each has 1 to 32 tokens.
All inputs are finite; a program needn't handle non-finite values.
Results may differ from a plain program's by a relative error of at most 0.012.
Values may be sent and summed in bfloat16 or wider, within the bound.
A program may use at most 192 MiB of HBM per device.

v0:
```python
import jax
import jax.numpy as jnp
from jax import lax
from jax.sharding import PartitionSpec as P

HEADS = 12
SEQ = 64
STEP = 10


EPS_NORM = 1e-05
BETA_ONE = 0.9
BETA_TWO = 0.999
ADAM_EPS = 1e-08
RATE_MATRIX = 0.05
RATE_VECTOR = 0.5
WEIGHT_DECAY = 0.1
OUTER_RATE = 0.7
OUTER_MOMENTUM = 0.9
NEG_LARGE = -1e30


def norm_apply(values, gain, shift):
    centre = values - jnp.mean(values, axis=-1, keepdims=True)
    spread = jnp.mean(centre * centre, axis=-1, keepdims=True)
    return centre * lax.rsqrt(spread + EPS_NORM) * gain + shift


def gelu_tanh(values):
    return jax.nn.gelu(values, approximate=True)


def adam_step(weight, first, second, gradient, step_rate, weight_decay):
    first_new = BETA_ONE * first + (1.0 - BETA_ONE) * gradient
    second_new = BETA_TWO * second + (1.0 - BETA_TWO) * gradient * gradient
    first_hat = first_new / (1.0 - BETA_ONE**STEP)
    second_hat = second_new / (1.0 - BETA_TWO**STEP)
    local_weight = weight - step_rate * (
        first_hat / (jnp.sqrt(second_hat) + ADAM_EPS) + weight_decay * weight
    )
    return (first_new, second_new, weight - local_weight)


def local(
    inputs,
    segments,
    cotangent,
    attn_weight,
    attn_first,
    attn_second,
    attn_outer,
    mlp_weight,
    mlp_first,
    mlp_second,
    mlp_outer,
    vector_weight,
    vector_first,
    vector_second,
    vector_outer,
):
    bf16 = jnp.bfloat16
    f32 = jnp.float32
    attn_cast = attn_weight.astype(bf16)
    mlp_cast = mlp_weight.astype(bf16)
    attn_low, mlp_low, vector_low = (
        lax.all_gather(attn_cast, "fsdp", axis=0, tiled=True),
        lax.all_gather(mlp_cast, "fsdp", axis=1, tiled=True),
        lax.all_gather(vector_weight.astype(bf16), "fsdp", axis=1, tiled=True),
    )
    vectors = vector_low.astype(f32)
    tokens_f = inputs[0].astype(f32)
    seg_ids = segments[0]
    back_f = cotangent[0].astype(f32)
    model_width = attn_low.shape[0]
    head_dim = model_width // HEADS
    score_scale = head_dim ** (-0.5)
    tok_count = tokens_f.shape[0]
    row_count = tok_count // SEQ
    shape_four = (row_count, SEQ, HEADS, head_dim)
    normed_f, norm_pull = jax.vjp(norm_apply, tokens_f, vectors[0], vectors[1])
    normed = normed_f.astype(bf16)
    project = jnp.dot(normed, attn_low[:, : 3 * model_width], preferred_element_type=f32)
    queries = (project[:, :model_width] + vectors[2]).astype(bf16).reshape(shape_four)
    keys_all = project[:, model_width : 2 * model_width].astype(bf16).reshape(shape_four)
    values_all = (
        (project[:, 2 * model_width : 3 * model_width] + vectors[3])
        .astype(bf16)
        .reshape(shape_four)
    )
    scores = (
        jnp.einsum("rqhd,rkhd->rhqk", queries, keys_all, preferred_element_type=f32) * score_scale
    )
    same_seg = (seg_ids[:, :, None] == seg_ids[:, None, :])[:, None]
    masked = jnp.where(same_seg, scores, NEG_LARGE)
    exponent = jnp.exp(masked - jnp.max(masked, axis=-1, keepdims=True))
    soft = exponent / jnp.sum(exponent, axis=-1, keepdims=True)
    probs = soft.astype(bf16)
    mixed = (
        jnp.einsum("rhqk,rkhd->rqhd", probs, values_all, preferred_element_type=f32)
        .reshape(tok_count, model_width)
        .astype(bf16)
    )
    attended = (
        jnp.dot(mixed, attn_low[:, 3 * model_width :], preferred_element_type=f32) + vectors[4]
    )
    residual = tokens_f + attended
    normed_two_f, norm_two_pull = jax.vjp(norm_apply, residual, vectors[5], vectors[6])
    normed_two = normed_two_f.astype(bf16)
    up_pre = jnp.dot(normed_two, mlp_low[0], preferred_element_type=f32) + vectors[8:12].reshape(-1)
    hidden_f, gelu_pull = jax.vjp(gelu_tanh, up_pre)
    hidden = hidden_f.astype(bf16)
    branch = jnp.einsum("nf,df->nd", hidden, mlp_low[1], preferred_element_type=f32) + vectors[7]
    block_out = (residual + branch).astype(bf16)
    attn_low, mlp_low = (
        lax.all_gather(attn_cast, "fsdp", axis=0, tiled=True),
        lax.all_gather(mlp_cast, "fsdp", axis=1, tiled=True),
    )
    d_branch = cotangent[0]
    d_down_bias = jnp.sum(back_f, axis=0)
    grad_down = jnp.einsum("nd,nf->df", d_branch, hidden, preferred_element_type=f32)
    d_hidden = jnp.einsum("nd,df->nf", d_branch, mlp_low[1], preferred_element_type=f32)
    (d_up_f,) = gelu_pull(d_hidden)
    d_up = d_up_f.astype(bf16)
    d_up_bias = jnp.sum(d_up.astype(f32), axis=0)
    grad_up = jnp.einsum("nd,nf->df", normed_two, d_up, preferred_element_type=f32)
    mlp_grad = jnp.stack([grad_up, grad_down])
    d_normed_two = jnp.einsum("nf,df->nd", d_up, mlp_low[0], preferred_element_type=f32)
    d_res_norm, d_gain_two, d_shift_two = norm_two_pull(d_normed_two)
    d_res = back_f + d_res_norm
    d_att = d_res.astype(bf16)
    d_out_bias = jnp.sum(d_att.astype(f32), axis=0)
    grad_out = jnp.einsum("nc,nd->cd", mixed, d_att, preferred_element_type=f32)
    d_mixed = (
        jnp.einsum("nd,cd->nc", d_att, attn_low[:, 3 * model_width :], preferred_element_type=f32)
        .astype(bf16)
        .reshape(shape_four)
    )
    d_values = (
        jnp.einsum("rhqk,rqhd->rkhd", probs, d_mixed, preferred_element_type=f32)
        .reshape(tok_count, model_width)
        .astype(bf16)
    )
    d_probs = jnp.einsum("rqhd,rkhd->rhqk", d_mixed, values_all, preferred_element_type=f32)
    d_scores = (soft * (d_probs - jnp.sum(d_probs * soft, axis=-1, keepdims=True))).astype(bf16)
    d_queries = (
        (
            jnp.einsum("rhqk,rkhd->rqhd", d_scores, keys_all, preferred_element_type=f32)
            * score_scale
        )
        .reshape(tok_count, model_width)
        .astype(bf16)
    )
    d_keys = (
        (jnp.einsum("rhqk,rqhd->rkhd", d_scores, queries, preferred_element_type=f32) * score_scale)
        .reshape(tok_count, model_width)
        .astype(bf16)
    )
    d_query_bias = jnp.sum(d_queries.astype(f32), axis=0)
    d_value_bias = jnp.sum(d_values.astype(f32), axis=0)
    d_project = jnp.concatenate([d_queries, d_keys, d_values], axis=1)
    grad_qkv = jnp.einsum("nc,nd->cd", normed, d_project, preferred_element_type=f32)
    d_normed = jnp.einsum(
        "nd,cd->nc", d_project, attn_low[:, : 3 * model_width], preferred_element_type=f32
    )
    d_tok_norm, d_gain_one, d_shift_one = norm_pull(d_normed)
    input_grad = d_res + d_tok_norm
    attn_grad = jnp.concatenate([grad_qkv, grad_out], axis=1)
    vector_grad = jnp.concatenate(
        [
            jnp.stack(
                [
                    d_gain_one,
                    d_shift_one,
                    d_query_bias,
                    d_value_bias,
                    d_out_bias,
                    d_gain_two,
                    d_shift_two,
                    d_down_bias,
                ]
            ),
            d_up_bias.reshape(4, model_width),
        ],
        axis=0,
    )
    attn_sum, mlp_sum, vector_sum = (
        lax.psum_scatter(attn_grad, "fsdp", scatter_dimension=0, tiled=True),
        lax.psum_scatter(mlp_grad, "fsdp", scatter_dimension=1, tiled=True),
        lax.psum_scatter(vector_grad, "fsdp", scatter_dimension=1, tiled=True),
    )
    attn_moment, attn_square, attn_delta = adam_step(
        attn_weight, attn_first[0], attn_second[0], attn_sum, RATE_MATRIX, WEIGHT_DECAY
    )
    mlp_moment, mlp_square, mlp_delta = adam_step(
        mlp_weight, mlp_first[0], mlp_second[0], mlp_sum, RATE_MATRIX, WEIGHT_DECAY
    )
    vector_moment, vector_square, vector_delta = adam_step(
        vector_weight, vector_first[0], vector_second[0], vector_sum, RATE_VECTOR, 0.0
    )
    group_count = lax.axis_size("group")
    attn_total, mlp_total, vector_total = (
        lax.psum(attn_delta.astype(jnp.bfloat16), "group").astype(jnp.float32),
        lax.psum(mlp_delta.astype(jnp.bfloat16), "group").astype(jnp.float32),
        lax.psum(vector_delta.astype(jnp.bfloat16), "group").astype(jnp.float32),
    )
    attn_mean = attn_total / group_count
    mlp_mean = mlp_total / group_count
    vector_mean = vector_total / group_count
    attn_momentum = OUTER_MOMENTUM * attn_outer + attn_mean
    mlp_momentum = OUTER_MOMENTUM * mlp_outer + mlp_mean
    vector_momentum = OUTER_MOMENTUM * vector_outer + vector_mean
    attn_master = attn_weight - OUTER_RATE * (attn_mean + OUTER_MOMENTUM * attn_momentum)
    mlp_master = mlp_weight - OUTER_RATE * (mlp_mean + OUTER_MOMENTUM * mlp_momentum)
    vector_master = vector_weight - OUTER_RATE * (vector_mean + OUTER_MOMENTUM * vector_momentum)
    return (
        block_out[None],
        input_grad[None],
        attn_moment[None],
        attn_square[None],
        attn_momentum,
        attn_master,
        mlp_moment[None],
        mlp_square[None],
        mlp_momentum,
        mlp_master,
        vector_moment[None],
        vector_square[None],
        vector_momentum,
        vector_master,
    )


def solution(mesh):
    in_specs = (
        P("group", "fsdp", None),
        P("group", "fsdp", None),
        P("group", "fsdp", None),
        P("fsdp", None),
        P("group", "fsdp", None),
        P("group", "fsdp", None),
        P("fsdp", None),
        P(None, "fsdp", None),
        P("group", None, "fsdp", None),
        P("group", None, "fsdp", None),
        P(None, "fsdp", None),
        P(None, "fsdp"),
        P("group", None, "fsdp"),
        P("group", None, "fsdp"),
        P(None, "fsdp"),
    )
    out_specs = (
        P("group", "fsdp", None),
        P("group", "fsdp", None),
        P("group", "fsdp", None),
        P("group", "fsdp", None),
        P("fsdp", None),
        P("fsdp", None),
        P("group", None, "fsdp", None),
        P("group", None, "fsdp", None),
        P(None, "fsdp", None),
        P(None, "fsdp", None),
        P("group", None, "fsdp"),
        P("group", None, "fsdp"),
        P(None, "fsdp"),
        P(None, "fsdp"),
    )
    return jax.shard_map(local, mesh=mesh, in_specs=in_specs, out_specs=out_specs, check_vma=False)
```

profile of v0, /device:TPU:0, one launch (start us, length us, event | category | flops | bytes accessed | tf_op | source)
XLA Modules:
  0.0 981.9 jit_solution(8732145711654099097)
XLA Ops:
  12.5 32.4 %all-gather = bf16[8,96,12]{1,2,0:T(8,128)(2,1)S(1)} all-gather(bf16[1,96,12]{1,2,0:T(8,128)(2,1)S(1)} %convert_bitcast_fusion.2), channel_id=1, replica_groups=mesh['group'=4,'fsdp'=8] {'fsdp'}, dimensions={0}, use_global_device_ids=true | all-gather | bytes 20736 | tf_op jit(solution)/shard_map/all_gather | solution.py:68
  49.1 44.5 %all-gather.4.cloned.1.call-done = bf16[768,3072]{1,0:T(8,128)(2,1)} async-done(((bf16[96,3072]{1,0:T(8,128)(2,1)}), bf16[768,3072]{1,0:T(8,128)(2,1)}) %all-gather.4.cloned.1.call-update) | async-done | bytes 4718608 | tf_op jit(solution)/shard_map/all_gather | solution.py:66
  93.6 6.3 fusion.34
  103.5 5.9 reshape.167
  109.4 5.9 reshape.168
  115.3 6.5 copy.143
  121.8 5.9 reshape.157
  141.4 5.4 convert_element_type.140
  152.3 80.3 %all-gather.6.cloned.1.call-done = bf16[2,768,3072]{2,1,0:T(8,128)(2,1)} async-done(((bf16[2,96,3072]{2,1,0:T(8,128)(2,1)}), bf16[2,768,3072]{2,1,0:T(8,128)(2,1)}) %all-gather.6.cloned.1.call-update) | async-done | bytes 9437200 | tf_op jit(solution)/shard_map/all_gather | solution.py:67
  232.6 11.3 %fusion.10 = f32[1024,3072]{1,0:T(8,128)} fusion(bf16[2,768,3072]{2,1,0:T(8,128)(2,1)} %all-gather.6.cloned.1.call-done, f32[1024,768]{0,1:T(8,128)} %copy-done.2, f32[768]{0:T(1024)S(1)} %get-tuple-element.76, f32[768]{0:T(1024)S(1)} %get-tuple-element.74, f32[1024]{0:T(1024)S(1)} %fusion.67, f32[1024]{0:T(1024)S(1)} %broadcast_multiply_fusion), kind=kOutput, calls=%fused_computation.30 | convolution fusion | flops 4835770368 | bytes 20461568 | tf_op jit(solution)/shard_map/dot_general | solution.py:109
  243.9 14.4 %convert_reduce_fusion = (f32[3072]{0:T(1024)S(1)}, bf16[1024,3072]{1,0:T(8,128)(2,1)S(1)}) fusion(f32[1024,3072]{1,0:T(8,128)} %fusion.10, f32[3072]{0:T(1024)S(1)} %add.202, bf16[2,768,3072]{2,1,0:T(8,128)(2,1)S(1)} %copy-done.29, bf16[1,1024,768]{2,1,0:T(8,128)(2,1)S(1)} %copy-done.13), kind=kOutput, calls=%fused_computation.11 | convolution fusion | flops 4904186880 | bytes 25190400 | tf_op jit(solution)/shard_map/nd,df->nf/dot_general | solution.py:121
  258.4 6.7 fusion.83
  280.8 6.3 reshape.158
  287.1 9.9 %multiply_reduce_fusion = (f32[16,12,64]{2,1,0:T(8,128)S(1)}, f32[16,12,64,64]{2,3,1,0:T(8,128)}) fusion(f32[16,12,64,64]{2,3,1,0:T(8,128)} %copy-done.9, f32[16,12,64]{2,1,0:T(8,128)S(1)} %get-tuple-element.107, bf16[16,64,12,64]{3,2,1,0:T(8,128)(2,1)} %reshape.167, bf16[16,64,12,64]{3,2,1,0:T(8,128)(2,1)} %reshape.158), kind=kOutput, calls=%fused_computation.19 | convolution fusion | flops 103010304 | bytes 9535488 | tf_op jit(solution)/shard_map/rqhd,rkhd->rhqk/dot_general | solution.py:143
  297.0 7.0 multiply_convert_fusion.3
  310.9 6.1 convert_reduce_fusion.1
  325.1 5.4 convert_element_type.152
  358.7 8.6 fusion.72
  367.3 8.6 pad_maximum_fusion.1
  376.0 8.4 convolution_bitcast_fusion.1
  384.4 8.7 convolution_bitcast_fusion
  393.1 6.8 pad_maximum_fusion
  400.2 9.1 fusion.82
  417.5 6.2 convert_reduce_fusion.3
  425.0 112.7 %reduce-scatter.6.cloned.1.call-done = f32[96,3072]{1,0:T(8,128)} async-done(((f32[768,3072]{1,0:T(8,128)}), f32[96,3072]{1,0:T(8,128)}) %reduce-scatter.6.cloned.1.call-update) | async-done | bytes 1179664 | tf_op jit(solution)/shard_map/reduce_scatter | solution.py:187
  542.3 311.5 %reduce-scatter.8.cloned.1.call-done = f32[2,96,3072]{2,1,0:T(8,128)} async-done(((f32[2,768,3072]{2,1,0:T(8,128)}), f32[2,96,3072]{2,1,0:T(8,128)}) %reduce-scatter.8.cloned.1.call-update) | async-done | bytes 2359312 | tf_op jit(solution)/shard_map/reduce_scatter | solution.py:188
  853.8 8.3 fusion.59
  862.1 10.2 %fusion.52 = bf16[1,1024,768]{1,2,0:T(8,128)(2,1)S(1)} fusion(f32[1024,768]{0,1:T(8,128)} %copy-done.2, f32[768]{0:T(1024)S(1)} %copy-done.28, bf16[2,768,3072]{2,1,0:T(8,128)(2,1)} %all-gather.6.cloned.1.call-done, f32[1024,3072]{1,0:T(8,128)} %fusion.10, f32[3072]{0:T(1024)S(1)} %add.202), kind=kOutput, calls=%fused_computation.97 | convolution fusion | flops 4865654784 | bytes 22035456 | tf_op jit(solution)/shard_map/nf,df->nd/dot_general | solution.py:112
  877.6 40.4 %reduce-scatter.10.cloned.1.call-done = f32[96,12]{1,0:T(8,128)} async-done(((f32[768,12]{1,0:T(8,128)}), f32[96,12]{1,0:T(8,128)}) %reduce-scatter.10.cloned.1.call-update) | async-done | bytes 4624
  920.2 5.6 psum.23
  926.4 39.8 %all-reduce.3.cloned.1.call-done = (bf16[96,3072]{1,0:T(8,128)(2,1)}, bf16[2,96,3072]{2,1,0:T(8,128)(2,1)}) async-done(((bf16[96,3072]{1,0:T(8,128)(2,1)}, bf16[2,96,3072]{2,1,0:T(8,128)(2,1)}), (bf16[96,3072]{1,0:T(8,128)(2,1)}, bf16[2,96,3072]{2,1,0:T(8,128)(2,1)})) %all-reduce.3.cloned.1.call-update) | async-done | bytes 1769488 | tf_op jit(solution)/shard_map/psum | solution.py:202
  969.1 5.6 multiply_subtract_fusion
  (142 shorter events, 116.3 us)
Async XLA Ops:
  7.2 5.3 copy-start.20
  7.2 86.4 %all-gather.4.cloned.1.call-start = ((), (), s32[]{:S(2)}) async-start(), calls=%async_computation.3 | async-start | bytes 5308416 | tf_op jit(solution)/shard_map/all_gather | solution.py:66
  9.4 35.6 %copy-start.12 = (bf16[1,1024,768]{2,1,0:T(8,128)(2,1)S(1)}, bf16[1,1024,768]{2,1,0:T(8,128)(2,1)}, u32[]{:S(2)}) copy-start(bf16[1,1024,768]{2,1,0:T(8,128)(2,1)} %param.15) | copy-start | bytes 4718596
  9.4 223.2 %all-gather.6.cloned.1.call-start = ((), (), s32[]{:S(2)}) async-start(), calls=%async_computation.4 | async-start | bytes 10616832 | tf_op jit(solution)/shard_map/all_gather | solution.py:67
  12.4 525.3 %reduce-scatter.6.cloned.1.call-start = ((), (), s32[]{:S(2)}) async-start(), calls=%async_computation.5 | async-start | bytes 10616832 | tf_op jit(solution)/shard_map/reduce_scatter | solution.py:187
  45.8 3.1 copy-start.24
  48.9 51.0 %copy-start.22 = (f32[1024]{0:T(1024)}, f32[1024]{0:T(1024)S(1)}, u32[]{:S(2)}) copy-start(f32[1024]{0:T(1024)S(1)} %fusion.24) | copy-start | bytes 12292
  134.5 2.7 copy-start.9
  232.6 11.3 %copy-start.13 = (bf16[1,1024,768]{2,1,0:T(8,128)(2,1)S(1)}, bf16[1,1024,768]{2,1,0:T(8,128)(2,1)}, u32[]{:S(2)}) copy-start(bf16[1,1024,768]{2,1,0:T(8,128)(2,1)} %param.17) | copy-start | bytes 4718596
  232.6 11.3 %copy-start.29 = (bf16[2,768,3072]{2,1,0:T(8,128)(2,1)S(1)}, bf16[2,768,3072]{2,1,0:T(8,128)(2,1)}, u32[]{:S(2)}) copy-start(bf16[2,768,3072]{2,1,0:T(8,128)(2,1)} %all-gather.6.cloned.1.call-done) | copy-start | bytes 28311556
  258.3 6.7 copy-start.30
  268.6 3.9 copy-start.3
  268.6 4.7 copy-start.5
  297.0 7.0 copy-start.6
  304.0 3.5 copy-start.1
  307.5 3.4 copy-start.11
  310.9 6.2 copy-start.15
  310.9 6.2 copy-start.17
  354.6 2.8 copy-start.8
  375.9 477.8 %reduce-scatter.8.cloned.1.call-start = ((), (), s32[]{:S(2)}) async-start(), calls=%async_computation.6 | async-start | bytes 21233664 | tf_op jit(solution)/shard_map/reduce_scatter | solution.py:188
  376.0 8.5 copy-start.14
  400.0 518.1 %reduce-scatter.10.cloned.1.call-start = ((), (), s32[]{:S(2)}) async-start(), calls=%async_computation.7 | async-start | bytes 442368
  412.8 3.1 copy-start
  424.7 541.5 %all-reduce.3.cloned.1.call-start = ((), (), s32[]{:S(2)}) async-start(), calls=%async_computation.8 | async-start | bytes 3538944 | tf_op jit(solution)/shard_map/psum | solution.py:202
  542.3 319.8 %copy-start.28 = (f32[768]{0:T(1024)S(1)}, f32[768]{0:T(1024)}, u32[]{:S(2)}) copy-start(f32[768]{0:T(1024)} %get-tuple-element.75) | copy-start | bytes 9220
  873.9 45.0 %copy-start.21 = (f32[12,96]{1,0:T(8,128)S(1)}, f32[12,96]{1,0:T(8,128)}, u32[]{:S(2)}) copy-start(f32[12,96]{1,0:T(8,128)} %param.26) | copy-start | bytes 13828
  873.9 45.0 %copy-start.26 = (f32[1,12,96]{2,0,1:T(1,128)S(1)}, f32[1,12,96]{2,0,1:T(1,128)}, u32[]{:S(2)}) copy-start(f32[1,12,96]{2,0,1:T(1,128)} %param.27) | copy-start | bytes 13828
  873.9 45.0 %copy-start.27 = (f32[1,12,96]{2,0,1:T(1,128)S(1)}, f32[1,12,96]{2,0,1:T(1,128)}, u32[]{:S(2)}) copy-start(f32[1,12,96]{2,0,1:T(1,128)} %param.28) | copy-start | bytes 13828
  873.9 51.9 %copy-start.25 = (f32[12,96]{1,0:T(8,128)S(1)}, f32[12,96]{1,0:T(8,128)}, u32[]{:S(2)}) copy-start(f32[12,96]{1,0:T(8,128)} %param.29) | copy-start | bytes 13828
  873.9 92.3 %copy-start.7 = (f32[96,3072]{1,0:T(8,128)S(1)}, f32[96,3072]{1,0:T(8,128)}, u32[]{:S(2)}) copy-start(f32[96,3072]{1,0:T(8,128)} %param.18) | copy-start | bytes 3538948
  873.9 92.3 %copy-start.18 = (f32[96,3072]{1,0:T(8,128)S(1)}, f32[96,3072]{1,0:T(8,128)}, u32[]{:S(2)}) copy-start(f32[96,3072]{1,0:T(8,128)} %param.21) | copy-start | bytes 3538948
  966.2 2.9 copy-start.19
  (5 other events, 9.8 us)
Sparse Core Ops, SparseCore 0:
  10.8 82.7 all-gather.3
  96.4 136.1 all-gather.5
  376.0 161.6 reduce-scatter.5
  541.4 312.2 reduce-scatter.7
  857.4 60.5 reduce-scatter.9
  920.9 45.2 all-reduce.2
where the time goes:
time: 991 us; the launch traced here: 982 us
  waiting for transfers between devices  629 us (63%)
  matrix products  123 us (12%)
  local copies, waits for them, and re-layouts  105 us (11%)
  other arithmetic  71.1 us (7%)
  blocking collectives  38 us (4%)
  between operations  15 us (2%)
    reduce_scatter x1, waiting for transfers between devices, local(): lax.psum_scatter(mlp_grad, 'fsdp', scatter_dimension=1, tiled=True)  311 us
    reduce_scatter x1, waiting for transfers between devices, local(): lax.psum_scatter(attn_grad, 'fsdp', scatter_dimension=0, tiled=True)  113 us
    all_gather x1, waiting for transfers between devices, local(): lax.all_gather(mlp_cast, 'fsdp', axis=1, tiled=True)  80.3 us
    all_gather x1, waiting for transfers between devices, local(): lax.all_gather(attn_cast, 'fsdp', axis=0, tiled=True)  44.5 us
    unnamed x7, waiting for transfers between devices  40.5 us
    psum x1, waiting for transfers between devices, local(): lax.psum(attn_delta.astype(jnp.bfloat16), 'group').astype(jnp.float32)  39.8 us
    all_gather x1, blocking collectives, local(): lax.all_gather(vector_weight.astype(bf16), 'fsdp', axis=1, tiled=True)  32.4 us
    unnamed x72, local copies, waits for them, and re-layouts  22.6 us
  transfers between devices with their start and end apart: 6, of which 6 were waited for; matrix products, arithmetic and copies ran while one was open for 14% of the time, Pallas kernels for 0%

commit v1 on v0

--- a/solution.py
+++ b/solution.py
@@ -111,10 +111,6 @@
     hidden = hidden_f.astype(bf16)
     branch = jnp.einsum("nf,df->nd", hidden, mlp_low[1], preferred_element_type=f32) + vectors[7]
     block_out = (residual + branch).astype(bf16)
-    attn_low, mlp_low = (
-        lax.all_gather(attn_cast, "fsdp", axis=0, tiled=True),
-        lax.all_gather(mlp_cast, "fsdp", axis=1, tiled=True),
-    )
     d_branch = cotangent[0]
     d_down_bias = jnp.sum(back_f, axis=0)
     grad_down = jnp.einsum("nd,nf->df", d_branch, hidden, preferred_element_type=f32)
@@ -184,8 +180,8 @@
         axis=0,
     )
     attn_sum, mlp_sum, vector_sum = (
-        lax.psum_scatter(attn_grad, "fsdp", scatter_dimension=0, tiled=True),
-        lax.psum_scatter(mlp_grad, "fsdp", scatter_dimension=1, tiled=True),
+        lax.psum_scatter(attn_grad.astype(bf16), "fsdp", scatter_dimension=0, tiled=True).astype(f32),
+        lax.psum_scatter(mlp_grad.astype(bf16), "fsdp", scatter_dimension=1, tiled=True).astype(f32),
         lax.psum_scatter(vector_grad, "fsdp", scatter_dimension=1, tiled=True),
     )
     attn_moment, attn_square, attn_delta = adam_step(

time: 991 us -> 761 us (0.77)
  waiting for transfers between devices: 629 us -> 403 us
    reduce_scatter x2, waiting for transfers between devices: 424 us -> 205 us  [the longest x1 162 us: local(): lax.psum_scatter(mlp_grad.astype(bf16), 'fsdp', scatter_dimension=1, tile...]
    unnamed x72 -> x78, local copies, waits for them, and re-layouts: 22.6 us -> 25.4 us
  transfers between devices with their start and end apart: 6 -> 6, of which waited for: 6 -> 6; matrix products, arithmetic and copies ran while one was open for 14% -> 19% of each run, Pallas kernels for 0% -> 0%
where the time goes in v1:
time: 761 us; the launch traced here: 752 us
  waiting for transfers between devices  403 us (53%)
  matrix products  121 us (16%)
  local copies, waits for them, and re-layouts  107 us (14%)
  other arithmetic  66.3 us (9%)
  blocking collectives  38 us (5%)
  between operations  15 us (2%)
    reduce_scatter x1, waiting for transfers between devices, local(): lax.psum_scatter(mlp_grad.astype(bf16), 'fsdp', scatter_dimension=1, tile...  162 us
    all_gather x1, waiting for transfers between devices, local(): lax.all_gather(mlp_cast, 'fsdp', axis=1, tiled=True)  73.6 us
    all_gather x1, waiting for transfers between devices, local(): lax.all_gather(attn_cast, 'fsdp', axis=0, tiled=True)  44.5 us
    reduce_scatter x1, waiting for transfers between devices, local(): lax.psum_scatter(attn_grad.astype(bf16), 'fsdp', scatter_dimension=0, til...  42.8 us
    unnamed x7, waiting for transfers between devices  40.7 us
    psum x1, waiting for transfers between devices, local(): lax.psum(attn_delta.astype(jnp.bfloat16), 'group').astype(jnp.float32)  39.8 us
    all_gather x1, blocking collectives, local(): lax.all_gather(vector_weight.astype(bf16), 'fsdp', axis=1, tiled=True)  32.4 us
    unnamed x78, local copies, waits for them, and re-layouts  25.4 us
  transfers between devices with their start and end apart: 6, of which 6 were waited for; matrix products, arithmetic and copies ran while one was open for 19% of the time, Pallas kernels for 0%

profile of v1, /device:TPU:0, one launch (start us, length us, event | category | flops | bytes accessed | tf_op | source)
XLA Modules:
  0.0 751.6 jit_solution(15650065874777139323)
XLA Ops:
  12.5 32.4 %all-gather = bf16[8,96,12]{1,2,0:T(8,128)(2,1)S(1)} all-gather(bf16[1,96,12]{1,2,0:T(8,128)(2,1)S(1)} %convert_bitcast_fusion.2), channel_id=1, replica_groups=mesh['group'=4,'fsdp'=8] {'fsdp'}, dimensions={0}, use_global_device_ids=true | all-gather | bytes 20736 | tf_op jit(solution)/shard_map/all_gather | solution.py:68
  49.1 44.5 %all-gather.4.cloned.1.call-done = bf16[768,3072]{1,0:T(8,128)(2,1)} async-done(((bf16[96,3072]{1,0:T(8,128)(2,1)}), bf16[768,3072]{1,0:T(8,128)(2,1)}) %all-gather.4.cloned.1.call-update) | async-done | bytes 4718608 | tf_op jit(solution)/shard_map/all_gather | solution.py:66
  93.6 6.3 fusion.36
  105.2 5.9 reshape.157
  116.1 5.9 reshape.168
  122.0 6.5 copy.143
  128.5 5.9 reshape.167
  148.0 5.6 convert_element_type.148
  159.0 73.6 %all-gather.6.cloned.1.call-done = bf16[2,768,3072]{2,1,0:T(8,128)(2,1)} async-done(((bf16[2,96,3072]{2,1,0:T(8,128)(2,1)}), bf16[2,768,3072]{2,1,0:T(8,128)(2,1)}) %all-gather.6.cloned.1.call-update) | async-done | bytes 9437200 | tf_op jit(solution)/shard_map/all_gather | solution.py:67
  232.6 11.2 %fusion.12 = f32[1024,3072]{1,0:T(8,128)} fusion(bf16[2,768,3072]{2,1,0:T(8,128)(2,1)} %all-gather.6.cloned.1.call-done, f32[1024,768]{0,1:T(8,128)} %copy-done.2, f32[768]{0:T(1024)S(1)} %get-tuple-element.76, f32[768]{0:T(1024)S(1)} %get-tuple-element.74, f32[1024]{0:T(1024)S(1)} %fusion.71, f32[1024]{0:T(1024)S(1)} %broadcast_multiply_fusion), kind=kOutput, calls=%fused_computation.33 | convolution fusion | flops 4835770368 | bytes 20461568 | tf_op jit(solution)/shard_map/dot_general | solution.py:109
  243.8 14.4 %convert_reduce_fusion = (f32[3072]{0:T(1024)S(1)}, bf16[1024,3072]{1,0:T(8,128)(2,1)S(1)}) fusion(f32[1024,3072]{1,0:T(8,128)} %fusion.12, f32[3072]{0:T(1024)S(1)} %add.202, bf16[2,768,3072]{2,1,0:T(8,128)(2,1)S(1)} %copy-done.32, bf16[1,1024,768]{2,1,0:T(8,128)(2,1)S(1)} %copy-done.16), kind=kOutput, calls=%fused_computation.10 | convolution fusion | flops 4904186880 | bytes 25190400 | tf_op jit(solution)/shard_map/nd,df->nf/dot_general | solution.py:117
  258.3 6.7 fusion.86
  283.0 6.3 reshape.158
  289.3 10.0 %multiply_reduce_fusion = (f32[16,12,64]{2,1,0:T(8,128)S(1)}, f32[16,12,64,64]{2,3,1,0:T(8,128)}) fusion(f32[16,12,64,64]{2,3,1,0:T(8,128)} %copy-done.12, f32[16,12,64]{2,1,0:T(8,128)S(1)} %get-tuple-element.107, bf16[16,64,12,64]{3,2,1,0:T(8,128)(2,1)} %reshape.167, bf16[16,64,12,64]{3,2,1,0:T(8,128)(2,1)} %reshape.158), kind=kOutput, calls=%fused_computation.18 | convolution fusion | flops 103010304 | bytes 9535488 | tf_op jit(solution)/shard_map/rqhd,rkhd->rhqk/dot_general | solution.py:139
  299.3 6.0 convert_reduce_fusion.1
  305.3 7.0 multiply_convert_fusion.3
  324.6 5.4 convert_element_type.166
  330.0 5.2 copy.146
  335.2 5.5 convert_element_type.163
  346.0 5.4 convert_element_type.160
  363.3 9.9 %fusion.9 = bf16[1,768,3072]{2,1,0:T(8,128)(2,1)} fusion(bf16[1024,3072]{1,0:T(8,128)(2,1)} %copy-done.33, f32[1024,768]{0,1:T(8,128)} %copy-done.2, f32[768]{0:T(1024)S(1)} %get-tuple-element.76, f32[768]{0:T(1024)S(1)} %get-tuple-element.74, f32[1024]{0:T(1024)S(1)} %fusion.71, f32[1024]{0:T(1024)S(1)} %broadcast_multiply_fusion), kind=kOutput, calls=%fused_computation.30 | convolution fusion | flops 4838129664 | bytes 14170112 | tf_op jit(solution)/shard_map/nd,nf->df/dot_general | solution.py:121
  373.2 10.4 %fusion.10 = bf16[1,768,3072]{2,1,0:T(8,128)(2,1)} fusion(bf16[1,1024,768]{2,1,0:T(8,128)(2,1)S(1)} %copy-done.17, f32[1024,3072]{1,0:T(8,128)} %fusion.12, f32[3072]{0:T(1024)S(1)} %add.202), kind=kOutput, calls=%fused_computation.31 | convolution fusion | flops 4865654784 | bytes 18886656 | tf_op jit(solution)/shard_map/nd,nf->df/dot_general | solution.py:116
  383.6 8.3 %pad_maximum_fusion = bf16[2,768,3072]{2,1,0:T(8,128)(2,1)} fusion(bf16[1,768,3072]{2,1,0:T(8,128)(2,1)} %fusion.10, bf16[1,768,3072]{2,1,0:T(8,128)(2,1)} %fusion.9), kind=kLoop, calls=%fused_computation.12 | loop fusion | flops 4718592 | bytes 18874368 | tf_op jit(solution)/shard_map/stack | solution.py:122
  392.4 9.0 %fusion.85 = (f32[768]{0:T(1024)S(1)}, f32[1024,768]{1,0:T(8,128)}) fusion(bf16[1024,2304]{0,1:T(8,128)(2,1)} %copy-done.22, bf16[768,3072]{1,0:T(8,128)(2,1)} %all-gather.4.cloned.1.call-done), kind=kOutput, calls=%fused_computation.158 | convolution fusion | flops 3624664320 | bytes 11406336 | tf_op jit(solution)/shard_map/nd,cd->nc/dot_general | solution.py:158
  414.2 42.8 %reduce-scatter.6.cloned.1.call-done = bf16[96,3072]{1,0:T(8,128)(2,1)} async-done(((bf16[768,3072]{1,0:T(8,128)(2,1)}), bf16[96,3072]{1,0:T(8,128)(2,1)}) %reduce-scatter.6.cloned.1.call-update) | async-done | bytes 589840 | tf_op jit(solution)/shard_map/reduce_scatter | solution.py:183
  461.4 162.1 %reduce-scatter.8.cloned.1.call-done = bf16[2,96,3072]{2,1,0:T(8,128)(2,1)} async-done(((bf16[2,768,3072]{2,1,0:T(8,128)(2,1)}), bf16[2,96,3072]{2,1,0:T(8,128)(2,1)}) %reduce-scatter.8.cloned.1.call-update) | async-done | bytes 1179664 | tf_op jit(solution)/shard_map/reduce_scatter | solution.py:184
  623.5 8.0 %fusion.57 = (f32[1,2,96,3072]{3,2,1,0:T(8,128)}, bf16[2,96,3072]{2,1,0:T(8,128)(2,1)}, f32[1,2,96,3072]{3,2,1,0:T(8,128)}) fusion(bf16[2,96,3072]{2,1,0:T(8,128)(2,1)} %reduce-scatter.8.cloned.1.call-done, f32[1,2,96,3072]{3,2,1,0:T(8,128)} %param.24, f32[2,96,3072]{2,1,0:T(8,128)} %param.22, f32[1,2,96,3072]{3,2,1,0:T(8,128)} %param.23), kind=kLoop, calls=%fused_computation.105 | loop fusion | flops 10616832 | bytes 14155776 | tf_op jit(solution)/shard_map/broadcast_in_dim | solution.py:219
  631.5 10.2 %fusion.55 = bf16[1,1024,768]{1,2,0:T(8,128)(2,1)S(1)} fusion(f32[1024,768]{0,1:T(8,128)} %copy-done.2, f32[768]{0:T(1024)S(1)} %copy-done.31, bf16[2,768,3072]{2,1,0:T(8,128)(2,1)} %all-gather.6.cloned.1.call-done, f32[1024,3072]{1,0:T(8,128)} %fusion.12, f32[3072]{0:T(1024)S(1)} %add.202), kind=kOutput, calls=%fused_computation.102 | convolution fusion | flops 4865654784 | bytes 22035456 | tf_op jit(solution)/shard_map/nf,df->nd/dot_general | solution.py:112
  647.1 40.6 %reduce-scatter.10.cloned.1.call-done = f32[96,12]{1,0:T(8,128)} async-done(((f32[768,12]{1,0:T(8,128)}), f32[96,12]{1,0:T(8,128)}) %reduce-scatter.10.cloned.1.call-update) | async-done | bytes 4624
  689.8 5.6 psum.23
  696.1 39.8 %all-reduce.3.cloned.1.call-done = (bf16[96,3072]{1,0:T(8,128)(2,1)}, bf16[2,96,3072]{2,1,0:T(8,128)(2,1)}) async-done(((bf16[96,3072]{1,0:T(8,128)(2,1)}, bf16[2,96,3072]{2,1,0:T(8,128)(2,1)}), (bf16[96,3072]{1,0:T(8,128)(2,1)}, bf16[2,96,3072]{2,1,0:T(8,128)(2,1)})) %all-reduce.3.cloned.1.call-update) | async-done | bytes 1769488 | tf_op jit(solution)/shard_map/psum | solution.py:198
  738.8 5.6 multiply_subtract_fusion
  (148 shorter events, 114.6 us)
Async XLA Ops:
  7.2 5.3 copy-start.23
  7.2 86.4 %all-gather.4.cloned.1.call-start = ((), (), s32[]{:S(2)}) async-start(), calls=%async_computation.3 | async-start | bytes 5308416 | tf_op jit(solution)/shard_map/all_gather | solution.py:66
  9.4 35.6 %copy-start.15 = (bf16[1,1024,768]{2,1,0:T(8,128)(2,1)S(1)}, bf16[1,1024,768]{2,1,0:T(8,128)(2,1)}, u32[]{:S(2)}) copy-start(bf16[1,1024,768]{2,1,0:T(8,128)(2,1)} %param.15) | copy-start | bytes 4718596
  9.4 223.2 %all-gather.6.cloned.1.call-start = ((), (), s32[]{:S(2)}) async-start(), calls=%async_computation.4 | async-start | bytes 10616832 | tf_op jit(solution)/shard_map/all_gather | solution.py:67
  12.4 444.5 %reduce-scatter.6.cloned.1.call-start = ((), (), s32[]{:S(2)}) async-start(), calls=%async_computation.5 | async-start | bytes 5308416 | tf_op jit(solution)/shard_map/reduce_scatter | solution.py:183
  45.8 3.1 copy-start.27
  48.9 51.0 %copy-start.25 = (f32[1024]{0:T(1024)}, f32[1024]{0:T(1024)S(1)}, u32[]{:S(2)}) copy-start(f32[1024]{0:T(1024)S(1)} %fusion.26) | copy-start | bytes 12292
  99.9 4.0 copy-start.9
  138.5 2.6 copy-start.13
  232.6 11.2 %copy-start.16 = (bf16[1,1024,768]{2,1,0:T(8,128)(2,1)S(1)}, bf16[1,1024,768]{2,1,0:T(8,128)(2,1)}, u32[]{:S(2)}) copy-start(bf16[1,1024,768]{2,1,0:T(8,128)(2,1)} %param.17) | copy-start | bytes 4718596
  232.6 11.2 %copy-start.32 = (bf16[2,768,3072]{2,1,0:T(8,128)(2,1)S(1)}, bf16[2,768,3072]{2,1,0:T(8,128)(2,1)}, u32[]{:S(2)}) copy-start(bf16[2,768,3072]{2,1,0:T(8,128)(2,1)} %all-gather.6.cloned.1.call-done) | copy-start | bytes 28311556
  258.3 6.7 copy-start.33
  268.6 3.9 copy-start.3
  268.6 4.7 copy-start.6
  289.3 10.0 %copy-start.14 = (bf16[16,64,12,64]{3,2,1,0:T(8,128)(2,1)S(1)}, bf16[16,64,12,64]{3,2,1,0:T(8,128)(2,1)}, u32[]{:S(2)}) copy-start(bf16[16,64,12,64]{3,2,1,0:T(8,128)(2,1)} %reshape.158) | copy-start | bytes 4718596
  305.3 7.0 copy-start.7
  312.3 3.6 copy-start.1
  356.0 4.5 copy-start.19
  363.2 260.2 %reduce-scatter.8.cloned.1.call-start = ((), (), s32[]{:S(2)}) async-start(), calls=%async_computation.6 | async-start | bytes 10616832 | tf_op jit(solution)/shard_map/reduce_scatter | solution.py:184
  363.3 9.9 %copy-start.17 = (bf16[1,1024,768]{2,1,0:T(8,128)(2,1)S(1)}, bf16[1,1024,768]{2,1,0:T(8,128)(2,1)}, u32[]{:S(2)}) copy-start(bf16[1,1024,768]{2,1,0:T(8,128)(2,1)} %param.17) | copy-start | bytes 4718596
  391.9 295.8 %reduce-scatter.10.cloned.1.call-start = ((), (), s32[]{:S(2)}) async-start(), calls=%async_computation.7 | async-start | bytes 442368
  405.0 2.7 copy-start.26
  405.0 2.9 copy-start
  413.9 322.0 %all-reduce.3.cloned.1.call-start = ((), (), s32[]{:S(2)}) async-start(), calls=%async_computation.8 | async-start | bytes 3538944 | tf_op jit(solution)/shard_map/psum | solution.py:198
  461.4 170.2 %copy-start.31 = (f32[768]{0:T(1024)S(1)}, f32[768]{0:T(1024)}, u32[]{:S(2)}) copy-start(f32[768]{0:T(1024)} %get-tuple-element.75) | copy-start | bytes 9220
  643.4 45.2 %copy-start.24 = (f32[12,96]{1,0:T(8,128)S(1)}, f32[12,96]{1,0:T(8,128)}, u32[]{:S(2)}) copy-start(f32[12,96]{1,0:T(8,128)} %param.26) | copy-start | bytes 13828
  643.4 45.2 %copy-start.29 = (f32[1,12,96]{2,0,1:T(1,128)S(1)}, f32[1,12,96]{2,0,1:T(1,128)}, u32[]{:S(2)}) copy-start(f32[1,12,96]{2,0,1:T(1,128)} %param.27) | copy-start | bytes 13828
  643.4 45.2 %copy-start.30 = (f32[1,12,96]{2,0,1:T(1,128)S(1)}, f32[1,12,96]{2,0,1:T(1,128)}, u32[]{:S(2)}) copy-start(f32[1,12,96]{2,0,1:T(1,128)} %param.28) | copy-start | bytes 13828
  643.4 52.1 %copy-start.28 = (f32[12,96]{1,0:T(8,128)S(1)}, f32[12,96]{1,0:T(8,128)}, u32[]{:S(2)}) copy-start(f32[12,96]{1,0:T(8,128)} %param.29) | copy-start | bytes 13828
  643.4 92.5 %copy-start.8 = (f32[96,3072]{1,0:T(8,128)S(1)}, f32[96,3072]{1,0:T(8,128)}, u32[]{:S(2)}) copy-start(f32[96,3072]{1,0:T(8,128)} %param.18) | copy-start | bytes 3538948
  643.4 92.5 %copy-start.20 = (f32[96,3072]{1,0:T(8,128)S(1)}, f32[96,3072]{1,0:T(8,128)}, u32[]{:S(2)}) copy-start(f32[96,3072]{1,0:T(8,128)} %param.21) | copy-start | bytes 3538948
  735.9 2.9 copy-start.21
  (8 other events, 17.0 us)
Sparse Core Ops, SparseCore 0:
  10.8 82.7 all-gather.3
  96.4 136.1 all-gather.5
  363.4 93.5 reduce-scatter.5
  460.4 163.0 reduce-scatter.7
  627.2 60.4 reduce-scatter.9
  690.6 45.2 all-reduce.2

commit v2 on v1

--- a/solution.py
+++ b/solution.py
@@ -1,14 +1,17 @@
+import functools
+
 import jax
 import jax.numpy as jnp
 from jax import lax
+from jax.experimental import pallas as pl
+from jax.experimental.pallas import tpu as pltpu
 from jax.sharding import PartitionSpec as P
 
+EPS_NORM = 1e-05
+NEG_LARGE = -1e30
 HEADS = 12
 SEQ = 64
 STEP = 10
-
-
-EPS_NORM = 1e-05
 BETA_ONE = 0.9
 BETA_TWO = 0.999
 ADAM_EPS = 1e-08
@@ -17,7 +20,1017 @@
 WEIGHT_DECAY = 0.1
 OUTER_RATE = 0.7
 OUTER_MOMENTUM = 0.9
-NEG_LARGE = -1e30
+
+
+MESH = pl.DeviceIdType.MESH
+BF = jnp.bfloat16
+F32 = jnp.float32
+D = 768
+FF = 3072
+T = 1024
+TB = 256
+SHARD = 96
+GELU_C = 0.7978845608028654
+GELU_A = 0.044715
+SCALE = 0.125
+
+
+def dot_nn(a, b):
+    return jnp.dot(a, b, preferred_element_type=F32)
+
+
+def dot_nt(a, b):
+    return lax.dot_general(a, b, (((1,), (1,)), ((), ())), preferred_element_type=F32)
+
+
+def dot_tn(a, b):
+    return lax.dot_general(a, b, (((0,), (0,)), ((), ())), preferred_element_type=F32)
+
+
+def coords():
+    g = lax.axis_index("group")
+    f = lax.axis_index("fsdp")
+    return g // 2, g % 2, f // 2, f % 2
+
+
+def dev(x, c, z, y):
+    return (2 * x + c, 2 * z + y)
+
+
+def remote(src, dst, ssem, rsem, to):
+    return pltpu.make_async_remote_copy(
+        src_ref=src, dst_ref=dst, send_sem=ssem, recv_sem=rsem, device_id=to, device_id_type=MESH
+    )
+
+
+def norm_parts(v):
+    centre = v - jnp.mean(v, axis=-1, keepdims=True)
+    spread = jnp.mean(centre * centre, axis=-1, keepdims=True)
+    scale = lax.rsqrt(spread + EPS_NORM)
+    return centre * scale, scale
+
+
+def head_masks():
+    lane = lax.broadcasted_iota(jnp.int32, (1, 128), 1)
+    low = (lane < 64).astype(F32).astype(BF)
+    high = (lane >= 64).astype(F32).astype(BF)
+    return low, high
+
+
+def segment_bias(seg_ref, i):
+    row = seg_ref[pl.ds(i, 1), :]
+    classes = lax.broadcasted_iota(jnp.int32, (16, 128), 0)
+    hot = (classes == row).astype(F32).astype(BF)
+    same = dot_tn(hot, hot)
+    bias = (same - 1.0) * (-NEG_LARGE)
+    return jnp.concatenate([bias, bias], axis=1)
+
+
+def soft_pair(q, k2, bias):
+    s = dot_nt(q, k2) * SCALE + bias
+    halves = []
+    for h in (0, 1):
+        part = s[:, 128 * h : 128 * h + 128]
+        e = jnp.exp(part - jnp.max(part, axis=-1, keepdims=True))
+        halves.append(e * (1.0 / jnp.sum(e, axis=-1, keepdims=True)))
+    return jnp.concatenate(halves, axis=1)
+
+
+def stack_heads(v, low, high):
+    return jnp.concatenate([v * low, v * high], axis=0)
+
+
+def gather_stages(w, sems, where):
+    x, c, z, y = where
+    ys, yr, us, ds, zr, xs, xr, cs, cr = sems
+    f = 2 * z + y
+    other = 2 * z + 1 - y
+
+    def rows(i):
+        return pl.ds(pl.multiple_of(i * SHARD, 32), SHARD)
+
+    def pair(i):
+        return pl.ds(pl.multiple_of(i * 2 * SHARD, 64), 2 * SHARD)
+
+    mine = 2 * x + c
+    across = 2 * (1 - x) + c
+    sib = 2 * x + 1 - c
+    sib_across = 2 * (1 - x) + 1 - c
+
+    def at(p, r, q):
+        return w.at[p // 2, r, pl.ds(pl.multiple_of(1536 * (p % 2) + 384 * q, 128), 384)]
+
+    def cp_y(p, r):
+        return remote(at(p, r, mine), at(p, r, mine), ys.at[p], yr.at[p], dev(x, c, z, 1 - y))
+
+    def cp_up(p, i):
+        return remote(at(p, pair(i), mine), at(p, pair(i), mine), us.at[p, i], zr.at[p, i], dev(x, c, z + 1, y))
+
+    def cp_down(p, i):
+        return remote(at(p, pair(i), mine), at(p, pair(i), mine), ds.at[p, i], zr.at[p, i], dev(x, c, z - 1, y))
+
+    def cp_x(p, r, i, q):
+        return remote(at(p, r, q), at(p, r, q), xs.at[p, i], xr.at[p, i], dev(1 - x, c, z, y))
+
+    def cp_c(p, r, i, q, k):
+        return remote(at(p, r, q), at(p, r, q), cs.at[p, 4 * k + i], cr.at[p, 4 * k + i], dev(x, 1 - c, z, y))
+
+    def others(fn):
+        for k in (1, 2, 3):
+            pl.when(z >= k)(functools.partial(fn, z - k))
+            pl.when(z + k <= 3)(functools.partial(fn, z + k))
+
+    def sa(p):
+        cp_y(p, rows(f)).start()
+
+    def sb(p):
+        cp_y(p, rows(other)).wait_recv()
+        pl.when(z < 3)(lambda: cp_up(p, z).start())
+        pl.when(z > 0)(lambda: cp_down(p, z).start())
+        cp_x(p, rows(other), z, mine).start()
+        cp_c(p, rows(other), z, mine, 0).start()
+
+    def hop(k, p):
+        def from_below():
+            i = z - k
+            cp_up(p, i).wait_recv()
+            pl.when(z < 3)(lambda: cp_up(p, i).start())
+            cp_x(p, pair(i), i, mine).start()
+            cp_c(p, pair(i), i, mine, 0).start()
+
+        def from_above():
+            i = z + k
+            cp_down(p, i).wait_recv()
+            pl.when(z > 0)(lambda: cp_down(p, i).start())
+            cp_x(p, pair(i), i, mine).start()
+            cp_c(p, pair(i), i, mine, 0).start()
+
+        pl.when(z >= k)(from_below)
+        pl.when(z + k <= 3)(from_above)
+
+    def sf(p):
+        cp_x(p, rows(other), z, across).wait_recv()
+        cp_c(p, rows(other), z, across, 1).start()
+
+        def fwd(i):
+            cp_x(p, pair(i), i, across).wait_recv()
+            cp_c(p, pair(i), i, across, 1).start()
+
+        others(fwd)
+
+    def sg(p):
+        cp_c(p, rows(other), z, sib, 0).wait_recv()
+        cp_c(p, rows(other), z, sib_across, 1).wait_recv()
+
+        def got(i):
+            cp_c(p, pair(i), i, sib, 0).wait_recv()
+            cp_c(p, pair(i), i, sib_across, 1).wait_recv()
+
+        others(got)
+
+    def drain(p):
+        cp_y(p, rows(f)).wait_send()
+        pl.when(z < 3)(lambda: cp_up(p, z).wait_send())
+        pl.when(z > 0)(lambda: cp_down(p, z).wait_send())
+        cp_x(p, rows(other), z, mine).wait_send()
+        cp_c(p, rows(other), z, mine, 0).wait_send()
+        cp_c(p, rows(other), z, across, 1).wait_send()
+        for k in (1, 2, 3):
+
+            @pl.when(z >= k)
+            def _():
+                pl.when(z < 3)(lambda: cp_up(p, z - k).wait_send())
+
+            @pl.when(z + k <= 3)
+            def _():
+                pl.when(z > 0)(lambda: cp_down(p, z + k).wait_send())
+
+        def sent(i):
+            cp_x(p, pair(i), i, mine).wait_send()
+            cp_c(p, pair(i), i, mine, 0).wait_send()
+            cp_c(p, pair(i), i, across, 1).wait_send()
+
+        others(sent)
+
+    stages = [sa, sb, functools.partial(hop, 1), functools.partial(hop, 2), functools.partial(hop, 3), sf, sg]
+    return stages, drain
+
+
+GATHER_SEMS = lambda n: [
+    pltpu.SemaphoreType.DMA((n,)),
+    pltpu.SemaphoreType.DMA((n,)),
+    pltpu.SemaphoreType.DMA((n, 4)),
+    pltpu.SemaphoreType.DMA((n, 4)),
+    pltpu.SemaphoreType.DMA((n, 4)),
+    pltpu.SemaphoreType.DMA((n, 4)),
+    pltpu.SemaphoreType.DMA((n, 4)),
+    pltpu.SemaphoreType.DMA((n, 8)),
+    pltpu.SemaphoreType.DMA((n, 8)),
+]
+PIECES = 6
+
+
+def forward_kernel(
+    x_in, cot_in, seg_in, aw, mw, vw,
+    w_out, qkvm_out, hid_out, gp_out, nrm_out, n2_out, res_out, xv_out, cotv_out, vec_out, seg_out,
+    w, xv, nrm, qkvm, res, n2, hid, gp, vec, seg, tiles, ub,
+    xsnd, xrcv, csnd, crcv, gsnd, grcv, vsnd, vrcv, osem,
+    *gsems,
+):
+    where = coords()
+    x, c, z, y = where
+    f = 2 * z + y
+    swapped = c != y
+    partner = dev(x, y, z, c)
+
+    barrier = pltpu.get_barrier_semaphore()
+
+    def greet(to):
+        pl.semaphore_signal(barrier, inc=1, device_id=to, device_id_type=MESH)
+
+    for k in range(1, 8):
+        greet((2 * x + c, (f + k) % 8))
+    greet(dev(x, 1 - c, z, y))
+    greet(dev(1 - x, c, z, y))
+    pl.when(swapped)(lambda: greet(partner))
+
+    own = pl.ds(pl.multiple_of(f * SHARD, 32), SHARD)
+    w[0, own, :] = aw[...].astype(BF)
+    w[1, own, :] = mw[0].astype(BF)
+    w[2, own, :] = mw[1].astype(BF)
+    tiles[pl.ds(f, 1)] = jnp.zeros((1, 16, 128), F32)
+    tiles[f, 0:12, 0:SHARD] = vw[...].astype(BF).astype(F32)
+
+    pl.semaphore_wait(barrier, 9 + swapped.astype(jnp.int32))
+
+    stages, drain = gather_stages(w, gsems, where)
+
+    def cp_vec(k, j):
+        return remote(tiles.at[j], tiles.at[j], vsnd.at[k - 1], vrcv.at[k - 1], (2 * x + c, (f + k) % 8))
+
+    def tok(b):
+        return pl.ds(pl.multiple_of(b * TB, TB), TB)
+
+    def x_remote(b):
+        return remote(x_in.at[tok(b)], xv.at[tok(b)], xsnd.at[b], xrcv.at[b], partner)
+
+    def x_local(b):
+        return pltpu.make_async_copy(x_in.at[tok(b)], xv.at[tok(b)], xrcv.at[b])
+
+    def cot_remote():
+        return remote(cot_in, cotv_out, csnd, crcv, partner)
+
+    def cot_local():
+        return pltpu.make_async_copy(cot_in, cotv_out, crcv)
+
+    def seg_remote():
+        return remote(seg_in, seg, gsnd, grcv, partner)
+
+    stages[0](0)
+    for k in range(1, 8):
+        cp_vec(k, f).start()
+
+    @pl.when(swapped)
+    def _():
+        seg_remote().start()
+        for b in range(4):
+            x_remote(b).start()
+
+    @pl.when(jnp.logical_not(swapped))
+    def _():
+        seg[...] = seg_in[...]
+        for b in range(4):
+            x_local(b).start()
+
+    outs = []
+
+    def write(src, dst):
+        cp = pltpu.make_async_copy(src, dst, osem.at[len(outs)])
+        cp.start()
+        outs.append(cp)
+
+    def tick(slot):
+        for p in range(PIECES):
+            s = slot - 2 * p
+            if 0 <= s <= 6 and (p, s) != (0, 0):
+                stages[s](p)
+                if s == 6 and p % 2 == 1:
+                    write(w.at[p // 2], w_out.at[p // 2])
+
+    def vectors():
+        for k in range(1, 8):
+            cp_vec(k, (f + 8 - k) % 8).wait_recv()
+        total = jnp.zeros((16, D), F32)
+        r = lax.broadcasted_iota(jnp.int32, (128, D), 0)
+        q = lax.broadcasted_iota(jnp.int32, (128, D), 1)
+        for j in range(8):
+            pick = jnp.logical_and(q == r + SHARD * j, r < SHARD).astype(F32).astype(BF)
+            total = total + dot_nn(tiles[j].astype(BF), pick)
+        vec[...] = total
+        for k in range(4):
+            ub[0:1, D * k : D * k + D] = total[8 + k : 9 + k, :]
+
+    def first_norm(b):
+        @pl.when(swapped)
+        def _():
+            x_remote(b).wait_recv()
+
+        @pl.when(jnp.logical_not(swapped))
+        def _():
+            x_local(b).wait()
+
+        hat, _ = norm_parts(xv[tok(b), :].astype(F32))
+        nrm[tok(b), :] = (hat * vec[0:1, :] + vec[1:2, :]).astype(BF)
+
+    def blocks(fn):
+        def step(b, carry):
+            fn(b)
+            return carry
+
+        lax.fori_loop(0, 4, step, 0)
+
+    def queries_keys(b):
+        r = dot_nn(nrm[tok(b), :], w[0, :, 0:1536])
+        qkvm[tok(b), 0:D] = (r[:, 0:D] + vec[2:3, :]).astype(BF)
+        qkvm[tok(b), D : 2 * D] = r[:, D : 2 * D].astype(BF)
+
+    def values(b):
+        r = dot_nn(nrm[tok(b), :], w[0, :, 1536:2304])
+        qkvm[tok(b), 2 * D : 3 * D] = (r + vec[3:4, :]).astype(BF)
+
+    def attention(i):
+        low, high = head_masks()
+        bias = segment_bias(seg, i)
+        r = pl.ds(pl.multiple_of(i * 128, 128), 128)
+        for p in range(6):
+            col = 128 * p
+            q = qkvm[r, col : col + 128]
+            k2 = stack_heads(qkvm[r, D + col : D + col + 128], low, high)
+            v2 = stack_heads(qkvm[r, 2 * D + col : 2 * D + col + 128], low, high)
+            probs = soft_pair(q, k2, bias).astype(BF)
+            qkvm[r, 3 * D + col : 3 * D + col + 128] = dot_nn(probs, v2).astype(BF)
+
+    def attend(lo, hi):
+        def step(i, carry):
+            attention(i)
+            return carry
+
+        lax.fori_loop(lo, hi, step, 0)
+
+    def out_norm(b):
+        att = dot_nn(qkvm[tok(b), 3 * D :], w[0, :, 2304:3072]) + vec[4:5, :]
+        r = xv[tok(b), :].astype(F32) + att
+        res[tok(b), :] = r
+        hat, _ = norm_parts(r)
+        n2[tok(b), :] = (hat * vec[5:6, :] + vec[6:7, :]).astype(BF)
+
+    def up(half, b):
+        for k in range(2):
+            lo = 1536 * half + 768 * k
+            u = dot_nn(n2[tok(b), :], w[1, :, lo : lo + 768]) + ub[0:1, lo : lo + 768]
+            u2 = u * u
+            t = jnp.tanh(u * (GELU_C + (GELU_C * GELU_A) * u2))
+            h = 0.5 + 0.5 * t
+            out = u * h
+            hid[tok(b), lo : lo + 768] = out.astype(BF)
+            slope = h + out * (1.0 - h) * (2.0 * GELU_C + (6.0 * GELU_C * GELU_A) * u2)
+            gp[tok(b), lo : lo + 768] = slope.astype(BF)
+
+    for slot in range(0, 4):
+        tick(slot)
+    vectors()
+    blocks(first_norm)
+
+    @pl.when(swapped)
+    def _():
+        cot_remote().start()
+
+    @pl.when(jnp.logical_not(swapped))
+    def _():
+        cot_local().start()
+
+    tick(4)
+    tick(5)
+    write(xv, xv_out)
+    write(nrm, nrm_out)
+    tick(6)
+    blocks(queries_keys)
+    tick(7)
+    tick(8)
+    blocks(values)
+
+    @pl.when(swapped)
+    def _():
+        remote(seg_in, seg, gsnd, grcv, partner).wait_recv()
+
+    attend(0, 4)
+    tick(9)
+    attend(4, 8)
+    write(qkvm, qkvm_out)
+    tick(10)
+    blocks(out_norm)
+    write(res, res_out)
+    write(n2, n2_out)
+    tick(11)
+    blocks(functools.partial(up, 0))
+    tick(12)
+    blocks(functools.partial(up, 1))
+    write(hid, hid_out)
+    write(gp, gp_out)
+    for slot in range(13, 2 * PIECES + 5):
+        tick(slot)
+    vec_out[...] = vec[...]
+    seg_out[...] = seg[...]
+
+    for p in range(PIECES):
+        drain(p)
+    for k in range(1, 8):
+        cp_vec(k, f).wait_send()
+
+    @pl.when(swapped)
+    def _():
+        seg_remote().wait_send()
+        for b in range(4):
+            x_remote(b).wait_send()
+        cot_remote().wait()
+
+    @pl.when(jnp.logical_not(swapped))
+    def _():
+        cot_local().wait()
+
+    for cp in outs:
+        cp.wait()
+
+
+def forward(x, cot, seg, aw, mw, vw):
+    any_ = pl.BlockSpec(memory_space=pl.ANY)
+    vm = pl.BlockSpec(memory_space=pltpu.VMEM)
+    wide = jax.ShapeDtypeStruct((T, FF), BF)
+    slim = jax.ShapeDtypeStruct((T, D), BF)
+    dma = pltpu.SemaphoreType.DMA
+    return pl.pallas_call(
+        forward_kernel,
+        out_shape=(
+            jax.ShapeDtypeStruct((3, D, FF), BF), wide, wide, wide, slim, slim,
+            jax.ShapeDtypeStruct((T, D), F32), slim, slim,
+            jax.ShapeDtypeStruct((16, D), F32), jax.ShapeDtypeStruct((8, 128), jnp.int32),
+        ),
+        in_specs=[any_, any_, vm, vm, vm, vm],
+        out_specs=(any_,) * 9 + (vm, vm),
+        scratch_shapes=[
+            pltpu.VMEM((3, D, FF), BF), pltpu.VMEM((T, D), BF), pltpu.VMEM((T, D), BF), pltpu.VMEM((T, FF), BF),
+            pltpu.VMEM((T, D), F32), pltpu.VMEM((T, D), BF), pltpu.VMEM((T, FF), BF), pltpu.VMEM((T, FF), BF),
+            pltpu.VMEM((16, D), F32), pltpu.VMEM((8, 128), jnp.int32), pltpu.VMEM((8, 16, 128), F32),
+            pltpu.VMEM((1, FF), F32),
+            dma((4,)), dma((4,)), dma, dma, dma, dma, dma((7,)), dma((7,)), dma((12,)),
+            *GATHER_SEMS(PIECES),
+        ],
+        compiler_params=pltpu.CompilerParams(collective_id=1, has_side_effects=True, vmem_limit_bytes=60 * 2**20),
+        name="forward",
+    )(x, cot, seg, aw, mw, vw)
+
+
+RS = 12
+RING = 2
+
+
+def adam_parts(first, second, weight, gradient, rate, decay):
+    first_new = BETA_ONE * first + (1.0 - BETA_ONE) * gradient
+    second_new = BETA_TWO * second + (1.0 - BETA_TWO) * gradient * gradient
+    first_hat = first_new * (1.0 / (1.0 - BETA_ONE**STEP))
+    second_hat = second_new * (1.0 / (1.0 - BETA_TWO**STEP))
+    delta = rate * (first_hat / (jnp.sqrt(second_hat) + ADAM_EPS) + decay * weight)
+    return first_new, second_new, delta
+
+
+def backward_kernel(
+    w_in, qkvm_in, hid_in, gp_in, nrm_in, n2_in, res_in, xv_in, cotv_in, vec, seg,
+    aw, a1, a2, ao, mw, m1, m2, mo, vw, v1, v2, vo,
+    out_o, ig_o, am_o, as_o, ap_o, aq_o, mm_o, ms_o, mp_o, mq_o, vm_o, vs_o, vp_o, vq_o,
+    A, B, W, cot, n2, E, R, G, S, ZI, FIN, DL, IN, OUT, vg, ubs, vsl, vrc, vdl,
+    lsem, d2s, d2r, zs, zr, fs, fr, ls, lr, isem, osem, bos, bor, igs, igr, vss, vsr, vds, vdr,
+):
+    x, c, z, y = coords()
+    f = 2 * z + y
+    g = 2 * x + c
+    swapped = c != y
+    kept = jnp.logical_not(swapped)
+    partner = dev(x, y, z, c)
+
+    barrier = pltpu.get_barrier_semaphore()
+
+    def greet(to):
+        pl.semaphore_signal(barrier, inc=1, device_id=to, device_id_type=MESH)
+
+    me16 = c * 8 + f
+    for k in range(1, 16):
+        other = (me16 + k) % 16
+        greet((2 * x + other // 8, other % 8))
+    greet(dev(1 - x, c, z, y))
+    greet(dev(1 - x, 1 - c, z, y))
+
+    def tok(b):
+        return pl.ds(pl.multiple_of(b * TB, TB), TB)
+
+    def load(src, dst, k):
+        return pltpu.make_async_copy(src, dst, lsem.at[k])
+
+    ld_cot = load(cotv_in, cot, 0)
+    ld_hid = load(hid_in, A, 1)
+    ld_wd = load(w_in.at[2], W, 2)
+    ld_gp = load(gp_in, B, 3)
+    ld_res = load(res_in, R, 4)
+    ld_n2 = load(n2_in, n2, 5)
+    ld_wu = load(w_in.at[1], W, 6)
+    ld_wa = load(w_in.at[0], W, 7)
+    ld_qkvm = load(qkvm_in, A, 8)
+    ld_nrm = load(nrm_in, E, 9)
+    ld_xv = load(xv_in, cot, 10)
+    for cp in (ld_cot, ld_hid, ld_wd, ld_gp, ld_res, ld_n2):
+        cp.start()
+    vg[...] = jnp.zeros((16, D), F32)
+    vsl[...] = jnp.zeros((8, 16, 128), F32)
+    vdl[...] = jnp.zeros((4, 16, 128), F32)
+    pl.semaphore_wait(barrier, 17)
+
+    def blocks(fn, lo=0, hi=4):
+        def step(b, carry):
+            fn(b)
+            return carry
+
+        lax.fori_loop(lo, hi, step, 0)
+
+    def wide(i, n=768):
+        return pl.ds(pl.multiple_of(i * n, 128), n)
+
+    ones = jnp.ones((16, T), BF)
+
+    def gradient(lhs, rhs, slot):
+        out = dot_tn(lhs, rhs)
+        for j in range(8):
+            G[slot, j % 2, j // 2] = out[SHARD * j : SHARD * j + SHARD].astype(BF)
+
+    def t_down(v):
+        @pl.when(v == 0)
+        def _():
+            ld_cot.wait()
+            ld_hid.wait()
+            vg[7:8, :] = dot_nn(ones, cot[...])[0:1, :]
+
+        gradient(cot[...], A[:, wide(v)], v % RING)
+
+    def out_remote(b):
+        return remote(E.at[tok(b)], out_o.at[tok(b)], bos.at[b], bor.at[b], partner)
+
+    def out_local(b):
+        return pltpu.make_async_copy(E.at[tok(b)], out_o.at[tok(b)], bor.at[b])
+
+    def mlp_back(b):
+        for k in range(4):
+            lo = 768 * k
+            dh = dot_nn(cot[tok(b), :], W[:, lo : lo + 768])
+            B[tok(b), lo : lo + 768] = (dh * B[tok(b), lo : lo + 768].astype(F32)).astype(BF)
+        branch = dot_nt(A[tok(b), :], W[...])
+        E[tok(b), :] = (R[tok(b), :] + branch + vec[7:8, :]).astype(BF)
+        pl.when(swapped)(lambda: out_remote(b).start())
+        pl.when(kept)(lambda: out_local(b).start())
+
+    def t_mlp0():
+        ld_wd.wait()
+        ld_gp.wait()
+        ld_res.wait()
+        blocks(mlp_back, 0, 2)
+
+    def t_mlp1():
+        blocks(mlp_back, 2, 4)
+        ld_wu.start()
+        ld_qkvm.start()
+        ld_n2.wait()
+
+    def t_up(v):
+        u = v - 6
+        ubs[0:1, wide(u)] = dot_nn(ones, B[:, wide(u)])[0:1, :]
+        gradient(n2[...], B[:, wide(u)], v % RING)
+
+    def norm_back(dn, v, gain):
+        hat, scale = norm_parts(v)
+        e = dn * gain
+        d = (e - jnp.mean(e, axis=-1, keepdims=True) - hat * jnp.mean(e * hat, axis=-1, keepdims=True)) * scale
+        return d, jnp.sum(dn * hat, axis=0, keepdims=True), jnp.sum(dn, axis=0, keepdims=True)
+
+    def second_norm(b):
+        dn = dot_nt(B[tok(b), :], W[...])
+        d, dgain, dshift = norm_back(dn, R[tok(b), :], vec[5:6, :])
+        d = d + cot[tok(b), :].astype(F32)
+        R[tok(b), :] = d
+        B[tok(b), 3 * D :] = d.astype(BF)
+        vg[5:6, :] = vg[5:6, :] + dgain
+        vg[6:7, :] = vg[6:7, :] + dshift
+
+    def t_norm2():
+        for k in range(4):
+            vg[8 + k : 9 + k, :] = ubs[0:1, D * k : D * k + D]
+        ld_wu.wait()
+        blocks(second_norm)
+        ld_wa.start()
+        ld_xv.start()
+        for b in range(4):
+            pl.when(swapped)(lambda: out_remote(b).wait_send())
+            pl.when(kept)(lambda: out_local(b).wait())
+        ld_nrm.start()
+
+    def mixed_back(b):
+        A[tok(b), 3 * D :] = dot_nt(B[tok(b), 3 * D :], W[:, 3 * D :]).astype(BF)
+
+    def t_out():
+        ld_qkvm.wait()
+        vg[4:5, :] = dot_nn(ones, B[:, 3 * D :])[0:1, :]
+        gradient(A[:, 3 * D :], B[:, 3 * D :], 8 % RING)
+        ld_wa.wait()
+        blocks(mixed_back)
+
+    def attention_back(i):
+        low, high = head_masks()
+        lane = lax.broadcasted_iota(jnp.int32, (1, 128), 1) < 64
+        bias = segment_bias(seg, i)
+        r = pl.ds(pl.multiple_of(i * 128, 128), 128)
+        for p in range(6):
+            col = 128 * p
+            q = A[r, col : col + 128]
+            k2 = stack_heads(A[r, D + col : D + col + 128], low, high)
+            v2 = stack_heads(A[r, 2 * D + col : 2 * D + col + 128], low, high)
+            dm = A[r, 3 * D + col : 3 * D + col + 128]
+            soft = soft_pair(q, k2, bias)
+            dp = dot_nt(dm, v2)
+            both = dot_tn(soft.astype(BF), dm)
+            B[r, 2 * D + col : 2 * D + col + 128] = jnp.where(lane, both[:128], both[128:]).astype(BF)
+            halves = []
+            for h in (0, 1):
+                part = dp[:, 128 * h : 128 * h + 128]
+                so = soft[:, 128 * h : 128 * h + 128]
+                halves.append(so * (part - jnp.sum(part * so, axis=-1, keepdims=True)))
+            ds = jnp.concatenate(halves, axis=1).astype(BF)
+            B[r, col : col + 128] = (dot_nn(ds, k2) * SCALE).astype(BF)
+            both = dot_tn(ds, q) * SCALE
+            B[r, D + col : D + col + 128] = jnp.where(lane, both[:128], both[128:]).astype(BF)
+
+    def t_att(v):
+        lo = (v - 12) * 4
+        blocks(lambda i: attention_back(lo + i))
+
+    def t_qkv(v):
+        u = v - 14
+
+        @pl.when(u == 0)
+        def _():
+            ld_nrm.wait()
+            vg[2:3, :] = dot_nn(ones, B[:, 0:D])[0:1, :]
+            vg[3:4, :] = dot_nn(ones, B[:, 2 * D : 3 * D])[0:1, :]
+
+        gradient(E[...], B[:, wide(u)], (v - 5) % RING)
+
+    def ig_remote(b):
+        return remote(R.at[tok(b)], ig_o.at[tok(b)], igs.at[b], igr.at[b], partner)
+
+    def ig_local(b):
+        return pltpu.make_async_copy(R.at[tok(b)], ig_o.at[tok(b)], igr.at[b])
+
+    def first_norm_back(b):
+        dn = dot_nt(B[tok(b), : 3 * D], W[:, : 3 * D])
+        d, dgain, dshift = norm_back(dn, cot[tok(b), :].astype(F32), vec[0:1, :])
+        R[tok(b), :] = R[tok(b), :] + d
+        vg[0:1, :] = vg[0:1, :] + dgain
+        vg[1:2, :] = vg[1:2, :] + dshift
+        pl.when(swapped)(lambda: ig_remote(b).start())
+        pl.when(kept)(lambda: ig_local(b).start())
+
+    def cp_slice(j):
+        return remote(vsl.at[j], vrc.at[2 * z + c], vss.at[j], vsr.at[2 * z + c], (2 * x + y, j))
+
+    def each_slice(fn):
+        def step(j, carry):
+            pl.when(jnp.logical_or(swapped, j != f))(lambda: fn(j))
+            return carry
+
+        lax.fori_loop(0, 8, step, 0)
+
+    def t_norm1():
+        ld_xv.wait()
+        blocks(first_norm_back)
+        for j in range(8):
+            vsl[j, :, 0:SHARD] = vg[:, SHARD * j : SHARD * j + SHARD]
+
+        @pl.when(kept)
+        def _():
+            vrc[pl.ds(2 * z + c, 1)] = vsl[pl.ds(f, 1)]
+
+        each_slice(lambda j: cp_slice(j).start())
+
+    def cp_change(k):
+        return remote(vdl.at[g], vdl.at[g], vds.at[k], vdr.at[g], members[k])
+
+    def t_vec_adam():
+        def step(s, carry):
+            pl.when(jnp.logical_or(swapped, s != 2 * z + c))(
+                lambda: remote(vrc.at[s], vrc.at[s], vss.at[0], vsr.at[s], partner).wait_recv()
+            )
+            return carry
+
+        lax.fori_loop(0, 8, step, 0)
+        grad = jnp.sum(vrc[...], axis=0)[0:12, 0:SHARD]
+        mom, sq, delta = adam_parts(v1[...], v2[...], vw[...], grad, RATE_VECTOR, 0.0)
+        vm_o[...] = mom
+        vs_o[...] = sq
+        vdl[g, 0:12, 0:SHARD] = delta
+        for k in range(3):
+            cp_change(k).start()
+
+    def t_vec_outer():
+        for k in range(3):
+            remote(vdl.at[froms[k]], vdl.at[froms[k]], vds.at[k], vdr.at[froms[k]], members[k]).wait_recv()
+        mean = jnp.sum(vdl[...], axis=0)[0:12, 0:SHARD] * 0.25
+        mom = OUTER_MOMENTUM * vo[...] + mean
+        vp_o[...] = mom
+        vq_o[...] = vw[...] - OUTER_RATE * (mean + OUTER_MOMENTUM * mom)
+
+    members = [dev(x, 1 - c, z, y), dev(1 - x, c, z, y), dev(1 - x, 1 - c, z, y)]
+    froms = [2 * x + 1 - c, 2 * (1 - x) + c, 2 * (1 - x) + 1 - c]
+
+    def tasks(v):
+        pl.when(v < 4)(lambda: t_down(v))
+        pl.when(v == 4)(t_mlp0)
+        pl.when(v == 5)(t_mlp1)
+        pl.when(jnp.logical_and(v >= 6, v <= 9))(lambda: t_up(v))
+        pl.when(v == 10)(t_norm2)
+        pl.when(v == 11)(t_out)
+        pl.when(jnp.logical_and(v >= 12, v <= 13))(lambda: t_att(v))
+        pl.when(jnp.logical_and(v >= 14, v <= 16))(lambda: t_qkv(v))
+        pl.when(v == 17)(t_norm1)
+        pl.when(v == 19)(t_vec_adam)
+        pl.when(v == 21)(t_vec_outer)
+
+    def piece(v):
+        first = jnp.logical_and(v >= 0, v < 4)
+        second = jnp.logical_and(v >= 6, v < 10)
+        third = v == 11
+        fourth = jnp.logical_and(v >= 14, v < 17)
+        real = jnp.logical_or(jnp.logical_or(first, second), jnp.logical_or(third, fourth))
+        p = jnp.where(v < 4, v, jnp.where(v < 10, v - 2, jnp.where(v < 12, 8, v - 5)))
+        return real, p
+
+    def cp_core(p):
+        return remote(G.at[p % RING, 1 - c], S.at[p], d2s.at[p], d2r.at[p], dev(x, 1 - c, z, y))
+
+    def hop_up(p, t, k):
+        return remote(S.at[p, t], ZI.at[p, t - z - 1], zs.at[p, k], zr.at[p, t - z - 1], dev(x, c, z + 1, y))
+
+    def hop_down(p, t, k):
+        return remote(S.at[p, t], ZI.at[p, 5 - z + t], zs.at[p, k], zr.at[p, 5 - z + t], dev(x, c, z - 1, y))
+
+    def got(p, k):
+        remote(ZI.at[p, k], ZI.at[p, k], zs.at[p, 0], zr.at[p, k], partner).wait_recv()
+
+    def add_in(p, t, k):
+        got(p, k)
+        S[p, t] = (S[p, t].astype(F32) + ZI[p, k].astype(F32)).astype(BF)
+
+    def s0(p):
+        cp_core(p).start()
+
+    def s1(p):
+        cp_core(p).wait_recv()
+        for t in range(4):
+            S[p, t] = (S[p, t].astype(F32) + G[p % RING, c, t].astype(F32)).astype(BF)
+
+        @pl.when(z == 0)
+        def _():
+            for k, t in enumerate((3, 2, 1)):
+                hop_up(p, t, k).start()
+
+        @pl.when(z == 3)
+        def _():
+            for k, t in enumerate((0, 1, 2)):
+                hop_down(p, t, k).start()
+
+        cp_core(p).wait_send()
+
+    def s2(p):
+        @pl.when(z == 1)
+        def _():
+            for k, t in enumerate((3, 2)):
+                add_in(p, t, t - 1)
+                hop_up(p, t, k).start()
+
+        @pl.when(z == 2)
+        def _():
+            for k, t in enumerate((0, 1)):
+                add_in(p, t, 2 + t)
+                hop_down(p, t, k).start()
+
+    def s3(p):
+        @pl.when(z == 2)
+        def _():
+            add_in(p, 3, 1)
+            hop_up(p, 3, 2).start()
+
+        @pl.when(z == 1)
+        def _():
+            add_in(p, 0, 3)
+            hop_down(p, 0, 2).start()
+
+    def cp_final(p):
+        return remote(S.at[p, z], FIN.at[p], fs.at[p], fr.at[p], partner)
+
+    def col(p):
+        return pl.ds(pl.multiple_of(768 * jnp.where(p < 8, p % 4, (p + 3) % 4), 128), 768)
+
+    def state_loads(p, fn):
+        q = p % 2
+
+        @pl.when(p < 8)
+        def _():
+            m = 1 - p // 4
+            for k, src in enumerate((m1, m2, mw, mo)):
+                fn(pltpu.make_async_copy(src.at[m, :, col(p)], IN.at[q, k], isem.at[q, k]))
+
+        @pl.when(p >= 8)
+        def _():
+            for k, src in enumerate((a1, a2, aw, ao)):
+                fn(pltpu.make_async_copy(src.at[:, col(p)], IN.at[q, k], isem.at[q, k]))
+
+    def state_stores(p, ks, fn):
+        q = p % 2
+
+        @pl.when(p < 8)
+        def _():
+            m = 1 - p // 4
+            for k in ks:
+                dst = (mm_o, ms_o, mp_o, mq_o)[k]
+                fn(pltpu.make_async_copy(OUT.at[q, k], dst.at[m, :, col(p)], osem.at[q, k]))
+
+        @pl.when(p >= 8)
+        def _():
+            for k in ks:
+                dst = (am_o, as_o, ap_o, aq_o)[k]
+                fn(pltpu.make_async_copy(OUT.at[q, k], dst.at[:, col(p)], osem.at[q, k]))
+
+    def start(cp):
+        cp.start()
+
+    def wait(cp):
+        cp.wait()
+
+    def s4(p):
+        state_loads(p, start)
+        pl.when(z > 0)(lambda: add_in(p, z, 0))
+        pl.when(z < 3)(lambda: add_in(p, z, 4))
+
+        @pl.when(swapped)
+        def _():
+            cp_final(p).start()
+
+        @pl.when(kept)
+        def _():
+            FIN[p] = S[p, z]
+
+    def cp_delta(p, k):
+        return remote(DL.at[p, g], DL.at[p, g], ls.at[p, k], lr.at[p, g], members[k])
+
+    def s5(p):
+        pl.when(swapped)(lambda: cp_final(p).wait_recv())
+        state_loads(p, wait)
+        pl.when(p >= 2)(lambda: state_stores(p - 2, (0, 1), wait))
+        q = p % 2
+
+        def rows(i, carry):
+            r = pl.ds(pl.multiple_of(i * 32, 32), 32)
+            mom, sq, delta = adam_parts(
+                IN[q, 0, r, :], IN[q, 1, r, :], IN[q, 2, r, :], FIN[p, r, :].astype(F32), RATE_MATRIX, WEIGHT_DECAY
+            )
+            OUT[q, 0, r, :] = mom
+            OUT[q, 1, r, :] = sq
+            DL[p, g, r, :] = delta.astype(BF)
+            return carry
+
+        lax.fori_loop(0, 3, rows, 0)
+        for k in (1, 2, 0):
+            cp_delta(p, k).start()
+        state_stores(p, (0, 1), start)
+
+    def s6(p):
+        for k in range(3):
+            remote(DL.at[p, froms[k]], DL.at[p, froms[k]], ls.at[p, k], lr.at[p, froms[k]], members[k]).wait_recv()
+        pl.when(p >= 2)(lambda: state_stores(p - 2, (2, 3), wait))
+        q = p % 2
+
+        def rows(i, carry):
+            r = pl.ds(pl.multiple_of(i * 32, 32), 32)
+            total = DL[p, 0, r, :].astype(F32)
+            for k in (1, 2, 3):
+                total = total + DL[p, k, r, :].astype(F32)
+            mean = total * 0.25
+            mom = OUTER_MOMENTUM * IN[q, 3, r, :] + mean
+            OUT[q, 2, r, :] = mom
+            OUT[q, 3, r, :] = IN[q, 2, r, :] - OUTER_RATE * (mean + OUTER_MOMENTUM * mom)
+            return carry
+
+        lax.fori_loop(0, 3, rows, 0)
+        state_stores(p, (2, 3), start)
+
+    def slot(v, carry):
+        tasks(v)
+        for k, fn in ((0, s0), (1, s1), (2, s2), (3, s3), (6, s6), (4, s4), (5, s5)):
+            real, p = piece(v - k)
+            pl.when(real)(functools.partial(fn, p))
+        return carry
+
+    lax.fori_loop(0, 23, slot, 0)
+
+    def drain(p, carry):
+        @pl.when(jnp.logical_or(z == 0, z == 3))
+        def _():
+            for k in range(3):
+                remote(S.at[p, k], ZI.at[p, k], zs.at[p, k], zr.at[p, k], partner).wait_send()
+
+        @pl.when(jnp.logical_and(z > 0, z < 3))
+        def _():
+            for k in range(3):
+                remote(S.at[p, k], ZI.at[p, k], zs.at[p, k], zr.at[p, k], partner).wait_send()
+
+        pl.when(swapped)(lambda: cp_final(p).wait_send())
+        for k in range(3):
+            cp_delta(p, k).wait_send()
+        return carry
+
+    lax.fori_loop(0, RS, drain, 0)
+    for p in (RS - 2, RS - 1):
+        state_stores(jnp.int32(p), (0, 1, 2, 3), wait)
+    each_slice(lambda j: cp_slice(j).wait_send())
+    for k in range(3):
+        cp_change(k).wait_send()
+    for b in range(4):
+
+        @pl.when(swapped)
+        def _():
+            out_remote(b).wait_recv()
+            ig_remote(b).wait()
+
+        @pl.when(kept)
+        def _():
+            ig_local(b).wait()
+
+
+def backward(fwd, states):
+    any_ = pl.BlockSpec(memory_space=pl.ANY)
+    vm = pl.BlockSpec(memory_space=pltpu.VMEM)
+    dma = pltpu.SemaphoreType.DMA
+    attn = jax.ShapeDtypeStruct((SHARD, FF), F32)
+    mlp = jax.ShapeDtypeStruct((2, SHARD, FF), F32)
+    vect = jax.ShapeDtypeStruct((12, SHARD), F32)
+    return pl.pallas_call(
+        backward_kernel,
+        out_shape=(
+            jax.ShapeDtypeStruct((T, D), BF), jax.ShapeDtypeStruct((T, D), F32),
+            attn, attn, attn, attn, mlp, mlp, mlp, mlp, vect, vect, vect, vect,
+        ),
+        in_specs=[any_] * 9 + [vm, vm] + [any_] * 8 + [vm] * 4,
+        out_specs=(any_,) * 10 + (vm,) * 4,
+        scratch_shapes=[
+            pltpu.VMEM((T, FF), BF), pltpu.VMEM((T, FF), BF), pltpu.VMEM((D, FF), BF),
+            pltpu.VMEM((T, D), BF), pltpu.VMEM((T, D), BF), pltpu.VMEM((T, D), BF), pltpu.VMEM((T, D), F32),
+            pltpu.VMEM((RING, 2, 4, SHARD, 768), BF), pltpu.VMEM((RS, 4, SHARD, 768), BF),
+            pltpu.VMEM((RS, 5, SHARD, 768), BF), pltpu.VMEM((RS, SHARD, 768), BF),
+            pltpu.VMEM((RS, 4, SHARD, 768), BF),
+            pltpu.VMEM((2, 4, SHARD, 768), F32), pltpu.VMEM((2, 4, SHARD, 768), F32),
+            pltpu.VMEM((16, D), F32), pltpu.VMEM((1, FF), F32),
+            pltpu.VMEM((8, 16, 128), F32), pltpu.VMEM((8, 16, 128), F32), pltpu.VMEM((4, 16, 128), F32),
+            dma((11,)), dma((RS,)), dma((RS,)), dma((RS, 3)), dma((RS, 5)), dma((RS,)), dma((RS,)),
+            dma((RS, 3)), dma((RS, 4)), dma((2, 4)), dma((2, 4)), dma((4,)), dma((4,)), dma((4,)), dma((4,)),
+            dma((8,)), dma((8,)), dma((3,)), dma((4,)),
+        ],
+        compiler_params=pltpu.CompilerParams(collective_id=2, has_side_effects=True, vmem_limit_bytes=63 * 2**20),
+        name="backward",
+    )(*fwd, *states)
+
+
+def fast(
+    inputs, segments, cotangent,
+    attn_weight, attn_first, attn_second, attn_outer,
+    mlp_weight, mlp_first, mlp_second, mlp_outer,
+    vector_weight, vector_first, vector_second, vector_outer,
+):
+    seg = segments[0].reshape(8, 128) + 8 * (lax.broadcasted_iota(jnp.int32, (8, 128), 1) // SEQ)
+    fwd = forward(inputs[0], cotangent[0], seg, attn_weight, mlp_weight, vector_weight)
+    out = backward(
+        fwd,
+        (
+            attn_weight, attn_first[0], attn_second[0], attn_outer,
+            mlp_weight, mlp_first[0], mlp_second[0], mlp_outer,
+            vector_weight, vector_first[0], vector_second[0], vector_outer,
+        ),
+    )
+    lead = (1, 1, 1, 1, 0, 0, 1, 1, 0, 0, 1, 1, 0, 0)
+    return tuple(v[None] if k else v for v, k in zip(out, lead))
 
 
 def norm_apply(values, gain, shift):
@@ -260,4 +1273,5 @@
         P(None, "fsdp"),
         P(None, "fsdp"),
     )
-    return jax.shard_map(local, mesh=mesh, in_specs=in_specs, out_specs=out_specs, check_vma=False)
+    fits = mesh.shape["group"] == 4 and mesh.shape["fsdp"] == 8
+    return jax.shard_map(fast if fits else local, mesh=mesh, in_specs=in_specs, out_specs=out_specs, check_vma=False)

time: 761 us -> 337 us (0.44); the launches traced: 752 us -> 336 us
  waiting for transfers between devices: 403 us -> 0 us
  Pallas kernels: 0 us -> 308 us
  matrix products: 121 us -> 0 us
  local copies, waits for them, and re-layouts: 107 us -> 26.9 us
  other arithmetic: 66.3 us -> 0.61 us
  blocking collectives: 38 us -> 0 us
  between operations: 15 us -> 0.69 us
    pallas_call x0 -> x2, Pallas kernels: none -> 308 us  [the longest x1 199 us: backward(): pl.pallas_call(backward_kernel, out_shape=(jax.ShapeDtypeStruct((T, D), B...]
    reduce_scatter x2 -> x0, waiting for transfers between devices: 205 us -> none  [the longest x1 162 us: local(): lax.psum_scatter(mlp_grad.astype(bf16), 'fsdp', scatter_dimension=1, tile...]
    dot_general x18 -> x0, matrix products: 121 us -> none  [the longest x1 14.4 us: local(): jnp.einsum('nd,df->nf', d_branch, mlp_low[1], preferred_element_type=f32)]
    all_gather x2 -> x0, waiting for transfers between devices: 118 us -> none  [the longest x1 73.6 us: local(): lax.all_gather(mlp_cast, 'fsdp', axis=1, tiled=True)]
    convert_element_type x9 -> x0, local copies, waits for them, and re-layouts: 41.8 us -> none  [the longest x2 10.8 us: local(): d_keys = (jnp.einsum('rhqk,rqhd->rkhd', d_scores, queries, preferred_elem...]
    unnamed x7 -> x0, waiting for transfers between devices: 40.7 us -> none
    psum x1 -> x0, waiting for transfers between devices: 39.8 us -> none  [local(): lax.psum(attn_delta.astype(jnp.bfloat16), 'group').astype(jnp.float32)]
    all_gather x1 -> x0, blocking collectives: 32.4 us -> none  [local(): lax.all_gather(vector_weight.astype(bf16), 'fsdp', axis=1, tiled=True)]
  transfers between devices with their start and end apart: 6 -> 0, of which waited for: 6 -> 0; matrix products, arithmetic and copies ran while one was open for 19% -> 0% of each run, Pallas kernels for 0% -> 0%
where the time goes in v2:
time: 337 us; the launch traced here: 336 us
  Pallas kernels  308 us (91%)
  local copies, waits for them, and re-layouts  26.9 us (8%)
    pallas_call x1, Pallas kernels, backward(): pl.pallas_call(backward_kernel, out_shape=(jax.ShapeDtypeStruct((T, D), B...  199 us
    pallas_call x1, Pallas kernels, forward(): pl.pallas_call(forward_kernel, out_shape=(jax.ShapeDtypeStruct((3, D, FF)...  109 us
    unnamed x37, local copies, waits for them, and re-layouts  26.1 us

profile of v2, /device:TPU:0, one launch (start us, length us, event | category | flops | bytes accessed | tf_op | source)
XLA Modules:
  0.0 335.9 jit_solution(8320942263600435789)
XLA Ops:
  0.7 0.8 reshape_squeeze.3
  1.4 0.6 multiply_add_fusion.seg_in
  2.0 1.3 copy_bitcast_fusion
  3.3 108.7 %forward.1 = (bf16[3,768,3072]{2,1,0:T(8,128)(2,1)}, bf16[1024,3072]{1,0:T(8,128)(2,1)}, bf16[1024,3072]{1,0:T(8,128)(2,1)}, bf16[1024,3072]{1,0:T(8,128)(2,1)},...) custom-call(bf16[1024,768]{1,0:T(8,128)(2,1)} %bitcast.24, ...), custom_call_target="tpu_custom_call" | custom-call | tf_op jit(solution)/shard_map/forward/pallas_call | solution.py:471
  112.0 199.1 %backward.1 = (bf16[1024,768]{1,0:T(8,128)(2,1)}, f32[1024,768]{1,0:T(8,128)}, f32[96,3072]{1,0:T(8,128)}, f32[96,3072]{1,0:T(8,128)}, f32[96,3072]{1,0:T(8,128)...) custom-call(bf16[3,768,3072]{2,1,0:T(8,128)(2,1)} %get-tuple-element, ...), custom_call_target="tpu_custom_call" | custom-call | tf_op jit(solution)/shard_map/backward/pallas_call | solution.py:990
  311.1 1.3 copy.29
  312.4 1.3 copy.30
  313.7 0.0 copy-start
  313.7 2.8 copy.47
  316.5 0.0 copy-done
  316.5 0.0 copy-start.8
  316.5 1.7 copy.48
  318.2 0.4 copy-done.8
  318.6 1.0 copy.49
  319.6 0.7 copy-done.7
  320.3 1.0 copy.50
  321.3 0.7 copy-done.6
  322.0 1.0 copy.51
  323.0 0.7 copy-done.5
  323.7 1.0 copy.52
  324.7 1.1 copy-done.4
  325.8 1.4 copy.53
  327.2 1.1 copy-done.3
  328.3 1.4 copy.54
  329.7 1.1 copy-done.2
  330.8 1.4 copy.55
  332.2 1.1 copy-done.1
  333.3 1.4 copy.56
  334.7 0.0 copy-done.10
  334.7 0.6 copy.57
  335.3 0.0 copy-done.9
  335.3 0.6 copy.58
  (11 shorter events, 0.0 us)
Async XLA Ops:
  313.7 2.8 copy-start
  316.5 2.1 copy-start.8
  318.6 1.7 copy-start.7
  320.3 1.7 copy-start.6
  322.0 1.7 copy-start.5
  323.7 2.1 copy-start.4
  325.8 2.5 copy-start.3
  328.3 2.5 copy-start.2
  330.8 2.5 copy-start.1
  333.3 1.4 copy-start.10
  333.3 2.0 copy-start.9

commit v3 on v2

--- a/solution.py
+++ b/solution.py
@@ -22,6 +22,38 @@
 OUTER_MOMENTUM = 0.9
 
 
+ORDER_FORWARD = (
+    ("cast", 0), ("g", 0, 0), ("g", 1, 0), ("xs", 3), ("cast", 1), ("g", 2, 0), ("vec", 0), ("g", 0, 1),
+    ("g", 1, 1), ("g", 0, 2), ("xs", 2), ("xs", 0), ("g", 3, 0), ("xs", 1), ("g", 2, 1), ("g", 0, 3), ("g", 1, 2),
+    ("g", 0, 4), ("g", 1, 3), ("cs", 0), ("g", 3, 1), ("g", 0, 5), ("g", 1, 4), ("g", 2, 2), ("g", 0, 6),
+    ("ln", 0, 4), ("qk", 0, 4), ("g", 1, 5), ("g", 2, 3), ("g", 1, 6), ("g", 3, 2), ("v", 0, 4), ("g", 2, 4),
+    ("at", 0, 2), ("g", 3, 3), ("at", 2, 2), ("g", 2, 5), ("g", 3, 4), ("on", 0, 4), ("g", 2, 6), ("u", 0, 0, 2),
+    ("g", 3, 5), ("u", 0, 2, 2), ("g", 3, 6), ("u", 1, 0, 2), ("u", 1, 2, 2), ("end", 0),
+)
+
+ORDER_BACKWARD = (
+    ("st", 0), ("g", 0, 0), ("gd", 0, 2), ("g", 0, 1), ("r", 1, 0), ("g", 1, 0), ("r", 0, 0), ("g", 1, 1),
+    ("g", 0, 2), ("r", 0, 1), ("r", 1, 1), ("gd", 2, 2), ("g", 0, 3), ("g", 1, 2), ("r", 2, 0), ("r", 0, 2),
+    ("g", 0, 4), ("g", 1, 3), ("r", 2, 1), ("il", 0), ("r", 3, 0), ("r", 0, 3), ("g", 1, 4), ("g", 0, 5),
+    ("r", 1, 2), ("r", 0, 4), ("r", 3, 1), ("g", 1, 5), ("il", 1), ("r", 1, 3), ("r", 0, 5), ("g", 1, 6),
+    ("g", 0, 6), ("dh", 0, 2), ("r", 1, 4), ("r", 2, 2), ("dh", 2, 2), ("r", 1, 5), ("gu", 0, 2), ("r", 4, 0),
+    ("r", 1, 6), ("r", 0, 6), ("r", 2, 3), ("r", 3, 2), ("r", 5, 0), ("r", 4, 1), ("r", 0, 7), ("r", 1, 7),
+    ("r", 2, 4), ("il", 2), ("r", 5, 1), ("r", 3, 3), ("gu", 2, 2), ("il", 3), ("r", 2, 5), ("r", 3, 4),
+    ("bo", 0, 4), ("r", 6, 0), ("r", 7, 0), ("r", 4, 2), ("r", 5, 2), ("r", 2, 6), ("ld", 0), ("r", 6, 1),
+    ("r", 3, 5), ("r", 2, 7), ("r", 4, 3), ("n2", 0, 2), ("r", 7, 1), ("r", 5, 3), ("r", 4, 4), ("il", 4),
+    ("r", 6, 2), ("r", 3, 6), ("n2", 2, 2), ("go", 0), ("ld", 1), ("r", 3, 7), ("r", 8, 0), ("r", 6, 3),
+    ("r", 5, 4), ("r", 4, 5), ("dm", 0, 4), ("r", 8, 1), ("r", 7, 2), ("il", 5), ("r", 5, 5), ("r", 4, 6),
+    ("ab", 0, 2), ("r", 6, 4), ("r", 4, 7), ("r", 8, 2), ("r", 7, 3), ("ab", 2, 2), ("r", 5, 6), ("r", 7, 4),
+    ("il", 6), ("r", 6, 5), ("gq", 0, 2), ("r", 9, 0), ("r", 8, 3), ("r", 10, 0), ("r", 5, 7), ("il", 7),
+    ("r", 7, 5), ("r", 9, 1), ("r", 6, 6), ("n1", 0, 2), ("r", 7, 6), ("r", 6, 7), ("r", 10, 1), ("il", 8),
+    ("r", 9, 2), ("r", 8, 4), ("n1", 2, 2), ("r", 10, 2), ("gq", 2, 1), ("r", 7, 7), ("r", 11, 0), ("r", 9, 3),
+    ("vs", 0), ("r", 8, 5), ("r", 11, 1), ("r", 9, 4), ("r", 10, 3), ("r", 11, 2), ("r", 8, 6), ("il", 9),
+    ("r", 10, 4), ("va", 0), ("r", 11, 3), ("r", 9, 5), ("vo", 0), ("r", 8, 7), ("il", 10), ("r", 11, 4),
+    ("r", 10, 5), ("r", 9, 6), ("r", 9, 7), ("il", 11), ("r", 11, 5), ("ic", 0), ("r", 10, 6), ("r", 11, 6),
+    ("r", 10, 7), ("r", 11, 7),
+)
+
+
 MESH = pl.DeviceIdType.MESH
 BF = jnp.bfloat16
 F32 = jnp.float32
@@ -100,7 +132,7 @@
     return jnp.concatenate([v * low, v * high], axis=0)
 
 
-def gather_stages(w, sems, where):
+def gather_stages(view, sems, where):
     x, c, z, y = where
     ys, yr, us, ds, zr, xs, xr, cs, cr = sems
     f = 2 * z + y
@@ -118,7 +150,7 @@
     sib_across = 2 * (1 - x) + 1 - c
 
     def at(p, r, q):
-        return w.at[p // 2, r, pl.ds(pl.multiple_of(1536 * (p % 2) + 384 * q, 128), 384)]
+        return view(p, r, pl.ds(pl.multiple_of(1536 * (p % 2) + 384 * q, 128), 384))
 
     def cp_y(p, r):
         return remote(at(p, r, mine), at(p, r, mine), ys.at[p], yr.at[p], dev(x, c, z, 1 - y))
@@ -227,13 +259,13 @@
     pltpu.SemaphoreType.DMA((n, 8)),
     pltpu.SemaphoreType.DMA((n, 8)),
 ]
-PIECES = 6
+PIECES = 4
 
 
 def forward_kernel(
-    x_in, cot_in, seg_in, aw, mw, vw,
+    x_in, cot_in, seg_raw, aw, mw, vw,
     w_out, qkvm_out, hid_out, gp_out, nrm_out, n2_out, res_out, xv_out, cotv_out, vec_out, seg_out,
-    w, xv, nrm, qkvm, res, n2, hid, gp, vec, seg, tiles, ub,
+    w, xv, nrm, qkvm, res, n2, hid, gp, vec, seg, seg_in, tiles, ub,
     xsnd, xrcv, csnd, crcv, gsnd, grcv, vsnd, vrcv, osem,
     *gsems,
 ):
@@ -254,22 +286,30 @@
     greet(dev(1 - x, c, z, y))
     pl.when(swapped)(lambda: greet(partner))
 
+    for i in range(8):
+        seg_in[i : i + 1, :] = jnp.concatenate([seg_raw[2 * i : 2 * i + 1, :], seg_raw[2 * i + 1 : 2 * i + 2, :] + 8], axis=1)
     own = pl.ds(pl.multiple_of(f * SHARD, 32), SHARD)
-    w[0, own, :] = aw[...].astype(BF)
-    w[1, own, :] = mw[0].astype(BF)
-    w[2, own, :] = mw[1].astype(BF)
     tiles[pl.ds(f, 1)] = jnp.zeros((1, 16, 128), F32)
     tiles[f, 0:12, 0:SHARD] = vw[...].astype(BF).astype(F32)
 
     pl.semaphore_wait(barrier, 9 + swapped.astype(jnp.int32))
 
-    stages, drain = gather_stages(w, gsems, where)
+    stages, drain = gather_stages(lambda p, r, q: w.at[p // 2, r, q], gsems, where)
 
     def cp_vec(k, j):
         return remote(tiles.at[j], tiles.at[j], vsnd.at[k - 1], vrcv.at[k - 1], (2 * x + c, (f + k) % 8))
 
-    def tok(b):
-        return pl.ds(pl.multiple_of(b * TB, TB), TB)
+    def tok(b, n=1):
+        if isinstance(b, int):
+            return pl.ds(b * TB, n * TB)
+        return pl.ds(pl.multiple_of(b * TB, TB), n * TB)
+
+    def span(fn, lo, n):
+        def step(b, carry):
+            fn(b)
+            return carry
+
+        lax.fori_loop(lo, lo + n, step, 0)
 
     def x_remote(b):
         return remote(x_in.at[tok(b)], xv.at[tok(b)], xsnd.at[b], xrcv.at[b], partner)
@@ -280,27 +320,8 @@
     def cot_remote():
         return remote(cot_in, cotv_out, csnd, crcv, partner)
 
-    def cot_local():
-        return pltpu.make_async_copy(cot_in, cotv_out, crcv)
-
     def seg_remote():
         return remote(seg_in, seg, gsnd, grcv, partner)
-
-    stages[0](0)
-    for k in range(1, 8):
-        cp_vec(k, f).start()
-
-    @pl.when(swapped)
-    def _():
-        seg_remote().start()
-        for b in range(4):
-            x_remote(b).start()
-
-    @pl.when(jnp.logical_not(swapped))
-    def _():
-        seg[...] = seg_in[...]
-        for b in range(4):
-            x_local(b).start()
 
     outs = []
 
@@ -309,13 +330,34 @@
         cp.start()
         outs.append(cp)
 
-    def tick(slot):
-        for p in range(PIECES):
-            s = slot - 2 * p
-            if 0 <= s <= 6 and (p, s) != (0, 0):
-                stages[s](p)
-                if s == 6 and p % 2 == 1:
-                    write(w.at[p // 2], w_out.at[p // 2])
+    def cast(m):
+        if m:
+            w[1, own, :] = mw[0].astype(BF)
+            return
+        w[0, own, :] = aw[...].astype(BF)
+        for k in range(1, 8):
+            cp_vec(k, f).start()
+
+        @pl.when(swapped)
+        def _():
+            seg_remote().start()
+
+        @pl.when(jnp.logical_not(swapped))
+        def _():
+            seg[...] = seg_in[...]
+            for b in range(4):
+                x_local(b).start()
+
+    def send_x(b):
+        pl.when(swapped)(lambda: x_remote(b).start())
+
+    def send_cot(k):
+        pl.when(swapped)(lambda: cot_remote().start())
+
+    def gather(p, s):
+        stages[s](p)
+        if s == 6 and p % 2 == 1:
+            write(w.at[p // 2], w_out.at[p // 2])
 
     def vectors():
         for k in range(1, 8):
@@ -342,13 +384,6 @@
         hat, _ = norm_parts(xv[tok(b), :].astype(F32))
         nrm[tok(b), :] = (hat * vec[0:1, :] + vec[1:2, :]).astype(BF)
 
-    def blocks(fn):
-        def step(b, carry):
-            fn(b)
-            return carry
-
-        lax.fori_loop(0, 4, step, 0)
-
     def queries_keys(b):
         r = dot_nn(nrm[tok(b), :], w[0, :, 0:1536])
         qkvm[tok(b), 0:D] = (r[:, 0:D] + vec[2:3, :]).astype(BF)
@@ -370,12 +405,14 @@
             probs = soft_pair(q, k2, bias).astype(BF)
             qkvm[r, 3 * D + col : 3 * D + col + 128] = dot_nn(probs, v2).astype(BF)
 
-    def attend(lo, hi):
-        def step(i, carry):
-            attention(i)
-            return carry
-
-        lax.fori_loop(lo, hi, step, 0)
+    greeted = []
+
+    def attend(lo, n):
+        if not greeted:
+            greeted.append(lo)
+            pl.when(swapped)(lambda: seg_remote().wait_recv())
+        span(attention, 2 * lo, 2 * n)
+        write(qkvm.at[tok(lo, n)], qkvm_out.at[tok(lo, n)])
 
     def out_norm(b):
         att = dot_nn(qkvm[tok(b), 3 * D :], w[0, :, 2304:3072]) + vec[4:5, :]
@@ -396,49 +433,27 @@
             slope = h + out * (1.0 - h) * (2.0 * GELU_C + (6.0 * GELU_C * GELU_A) * u2)
             gp[tok(b), lo : lo + 768] = slope.astype(BF)
 
-    for slot in range(0, 4):
-        tick(slot)
-    vectors()
-    blocks(first_norm)
-
-    @pl.when(swapped)
-    def _():
-        cot_remote().start()
-
-    @pl.when(jnp.logical_not(swapped))
-    def _():
-        cot_local().start()
-
-    tick(4)
-    tick(5)
-    write(xv, xv_out)
-    write(nrm, nrm_out)
-    tick(6)
-    blocks(queries_keys)
-    tick(7)
-    tick(8)
-    blocks(values)
-
-    @pl.when(swapped)
-    def _():
-        remote(seg_in, seg, gsnd, grcv, partner).wait_recv()
-
-    attend(0, 4)
-    tick(9)
-    attend(4, 8)
-    write(qkvm, qkvm_out)
-    tick(10)
-    blocks(out_norm)
-    write(res, res_out)
-    write(n2, n2_out)
-    tick(11)
-    blocks(functools.partial(up, 0))
-    tick(12)
-    blocks(functools.partial(up, 1))
-    write(hid, hid_out)
-    write(gp, gp_out)
-    for slot in range(13, 2 * PIECES + 5):
-        tick(slot)
+    def spanned(fn, *pairs):
+        def run(lo, n):
+            span(fn, lo, n)
+            for src, dst in pairs:
+                write(src.at[tok(lo, n)], dst.at[tok(lo, n)])
+
+        return run
+
+    def up_half(half, lo, n):
+        span(functools.partial(up, half), lo, n)
+        if half:
+            write(hid.at[tok(lo, n)], hid_out.at[tok(lo, n)])
+            write(gp.at[tok(lo, n)], gp_out.at[tok(lo, n)])
+
+    does = {
+        "g": gather, "cast": cast, "xs": send_x, "cs": send_cot, "vec": lambda k: vectors(),
+        "ln": spanned(first_norm, (xv, xv_out), (nrm, nrm_out)), "qk": spanned(queries_keys), "v": spanned(values),
+        "at": attend, "on": spanned(out_norm, (res, res_out), (n2, n2_out)), "u": up_half, "end": lambda k: None,
+    }
+    for name, *at in ORDER_FORWARD:
+        does[name](*at)
     vec_out[...] = vec[...]
     seg_out[...] = seg[...]
 
@@ -453,10 +468,6 @@
         for b in range(4):
             x_remote(b).wait_send()
         cot_remote().wait()
-
-    @pl.when(jnp.logical_not(swapped))
-    def _():
-        cot_local().wait()
 
     for cp in outs:
         cp.wait()
@@ -471,23 +482,63 @@
     return pl.pallas_call(
         forward_kernel,
         out_shape=(
-            jax.ShapeDtypeStruct((3, D, FF), BF), wide, wide, wide, slim, slim,
+            jax.ShapeDtypeStruct((2, D, FF), BF), wide, wide, wide, slim, slim,
             jax.ShapeDtypeStruct((T, D), F32), slim, slim,
             jax.ShapeDtypeStruct((16, D), F32), jax.ShapeDtypeStruct((8, 128), jnp.int32),
         ),
         in_specs=[any_, any_, vm, vm, vm, vm],
         out_specs=(any_,) * 9 + (vm, vm),
         scratch_shapes=[
-            pltpu.VMEM((3, D, FF), BF), pltpu.VMEM((T, D), BF), pltpu.VMEM((T, D), BF), pltpu.VMEM((T, FF), BF),
+            pltpu.VMEM((2, D, FF), BF), pltpu.VMEM((T, D), BF), pltpu.VMEM((T, D), BF), pltpu.VMEM((T, FF), BF),
             pltpu.VMEM((T, D), F32), pltpu.VMEM((T, D), BF), pltpu.VMEM((T, FF), BF), pltpu.VMEM((T, FF), BF),
-            pltpu.VMEM((16, D), F32), pltpu.VMEM((8, 128), jnp.int32), pltpu.VMEM((8, 16, 128), F32),
+            pltpu.VMEM((16, D), F32), pltpu.VMEM((8, 128), jnp.int32), pltpu.VMEM((8, 128), jnp.int32),
+            pltpu.VMEM((8, 16, 128), F32),
             pltpu.VMEM((1, FF), F32),
-            dma((4,)), dma((4,)), dma, dma, dma, dma, dma((7,)), dma((7,)), dma((12,)),
+            dma((4,)), dma((4,)), dma, dma, dma, dma, dma((7,)), dma((7,)), dma((40,)),
             *GATHER_SEMS(PIECES),
         ],
         compiler_params=pltpu.CompilerParams(collective_id=1, has_side_effects=True, vmem_limit_bytes=60 * 2**20),
         name="forward",
     )(x, cot, seg, aw, mw, vw)
+
+
+def final_kernel(*refs):
+    ins, small, outs, small_outs = refs[:10], refs[10:14], refs[14:24], refs[24:28]
+    bufs, rsem, wsem = refs[28:38], refs[38], refs[39]
+    reads = [pltpu.make_async_copy(a, b, rsem.at[k]) for k, (a, b) in enumerate(zip(ins, bufs))]
+    for cp in reads:
+        cp.start()
+    for k in range(4):
+        if k < 2:
+            for r in range(12):
+                small_outs[k][r] = small[k][r : r + 1, :]
+        else:
+            small_outs[k][...] = small[k][...]
+    writes = [pltpu.make_async_copy(b, a, wsem.at[k]) for k, (a, b) in enumerate(zip(outs, bufs))]
+    for r, w in zip(reads, writes):
+        r.wait()
+        w.start()
+    for w in writes:
+        w.wait()
+
+
+def finish(arrays):
+    any_ = pl.BlockSpec(memory_space=pl.ANY)
+    vm = pl.BlockSpec(memory_space=pltpu.VMEM)
+    big, small = arrays[:10], arrays[10:14]
+    shapes = [jax.ShapeDtypeStruct(a.shape, a.dtype) for a in big]
+    thin = jax.ShapeDtypeStruct((12, 1, SHARD), F32)
+    out = pl.pallas_call(
+        final_kernel,
+        out_shape=(*shapes, thin, thin, *[jax.ShapeDtypeStruct(a.shape, a.dtype) for a in small[2:]]),
+        in_specs=[any_] * 10 + [vm] * 4,
+        out_specs=(any_,) * 10 + (vm,) * 4,
+        scratch_shapes=[pltpu.VMEM(a.shape, a.dtype) for a in big]
+        + [pltpu.SemaphoreType.DMA((10,)), pltpu.SemaphoreType.DMA((10,))],
+        compiler_params=pltpu.CompilerParams(vmem_limit_bytes=63 * 2**20),
+        name="finish",
+    )(*big, *small)
+    return (*out[:10], jnp.transpose(out[10], (1, 0, 2)), jnp.transpose(out[11], (1, 0, 2)), out[12], out[13])
 
 
 RS = 12
@@ -504,11 +555,11 @@
 
 
 def backward_kernel(
-    w_in, qkvm_in, hid_in, gp_in, nrm_in, n2_in, res_in, xv_in, cotv_in, vec, seg,
+    cot_in, w_in, qkvm_in, hid_in, gp_in, nrm_in, n2_in, res_in, xv_in, cotv_in, vec, seg,
     aw, a1, a2, ao, mw, m1, m2, mo, vw, v1, v2, vo,
-    out_o, ig_o, am_o, as_o, ap_o, aq_o, mm_o, ms_o, mp_o, mq_o, vm_o, vs_o, vp_o, vq_o,
+    out_o, ig_o, am_o, as_o, ap_o, aq_o, mm_o, ms_o, mp_o, mq_o, vm_o, vs_o, vp_o, vq_o, ig_land,
     A, B, W, cot, n2, E, R, G, S, ZI, FIN, DL, IN, OUT, vg, ubs, vsl, vrc, vdl,
-    lsem, d2s, d2r, zs, zr, fs, fr, ls, lr, isem, osem, bos, bor, igs, igr, vss, vsr, vds, vdr,
+    lsem, d2s, d2r, zs, zr, fs, fr, ls, lr, isem, osem, bos, bor, igs, igr, vss, vsr, vds, vdr, *gsems,
 ):
     x, c, z, y = coords()
     f = 2 * z + y
@@ -529,15 +580,35 @@
     greet(dev(1 - x, c, z, y))
     greet(dev(1 - x, 1 - c, z, y))
 
-    def tok(b):
-        return pl.ds(pl.multiple_of(b * TB, TB), TB)
+    def tok(b, n=1):
+        if isinstance(b, int):
+            return pl.ds(b * TB, n * TB)
+        return pl.ds(pl.multiple_of(b * TB, TB), n * TB)
+
+    def span(fn, lo, n):
+        def step(b, carry):
+            fn(b)
+            return carry
+
+        lax.fori_loop(lo, lo + n, step, 0)
+
+    def spanned(fn, *cps):
+        def run(lo, n):
+            once(*cps)
+            span(fn, lo, n)
+
+        return run
+
+    own = pl.ds(pl.multiple_of(f * SHARD, 32), SHARD)
+    stages, gather_drain = gather_stages(lambda p, r, q: W.at[r, q], gsems, (x, c, z, y))
 
     def load(src, dst, k):
         return pltpu.make_async_copy(src, dst, lsem.at[k])
 
     ld_cot = load(cotv_in, cot, 0)
+    ld_own = load(cot_in, cot, 0)
     ld_hid = load(hid_in, A, 1)
-    ld_wd = load(w_in.at[2], W, 2)
+    ld_own_w = [load(mw.at[1, :, pl.ds(768 * k, 768)], IN.at[0, k], 11 + k) for k in range(4)]
     ld_gp = load(gp_in, B, 3)
     ld_res = load(res_in, R, 4)
     ld_n2 = load(n2_in, n2, 5)
@@ -546,22 +617,20 @@
     ld_qkvm = load(qkvm_in, A, 8)
     ld_nrm = load(nrm_in, E, 9)
     ld_xv = load(xv_in, cot, 10)
-    for cp in (ld_cot, ld_hid, ld_wd, ld_gp, ld_res, ld_n2):
+    pl.when(swapped)(lambda: ld_cot.start())
+    pl.when(kept)(lambda: ld_own.start())
+    for cp in (*ld_own_w, ld_hid, ld_gp, ld_res, ld_n2):
         cp.start()
     vg[...] = jnp.zeros((16, D), F32)
     vsl[...] = jnp.zeros((8, 16, 128), F32)
     vdl[...] = jnp.zeros((4, 16, 128), F32)
+    for k, cp in enumerate(ld_own_w):
+        cp.wait()
+        W[own, 768 * k : 768 * k + 768] = IN[0, k].astype(BF)
     pl.semaphore_wait(barrier, 17)
 
-    def blocks(fn, lo=0, hi=4):
-        def step(b, carry):
-            fn(b)
-            return carry
-
-        lax.fori_loop(lo, hi, step, 0)
-
     def wide(i, n=768):
-        return pl.ds(pl.multiple_of(i * n, 128), n)
+        return pl.ds(i * n if isinstance(i, int) else pl.multiple_of(i * n, n), n)
 
     ones = jnp.ones((16, T), BF)
 
@@ -570,14 +639,12 @@
         for j in range(8):
             G[slot, j % 2, j // 2] = out[SHARD * j : SHARD * j + SHARD].astype(BF)
 
-    def t_down(v):
-        @pl.when(v == 0)
-        def _():
+    def t_down(lo, n):
+        if lo == 0:
             ld_cot.wait()
             ld_hid.wait()
             vg[7:8, :] = dot_nn(ones, cot[...])[0:1, :]
-
-        gradient(cot[...], A[:, wide(v)], v % RING)
+        span(lambda v: gradient(cot[...], A[:, wide(v)], v % RING), lo, n)
 
     def out_remote(b):
         return remote(E.at[tok(b)], out_o.at[tok(b)], bos.at[b], bor.at[b], partner)
@@ -585,32 +652,53 @@
     def out_local(b):
         return pltpu.make_async_copy(E.at[tok(b)], out_o.at[tok(b)], bor.at[b])
 
-    def mlp_back(b):
+    waited = set()
+
+    def once(*cps):
+        for cp in cps:
+            if id(cp) not in waited:
+                waited.add(id(cp))
+                cp.wait()
+
+    def hidden_back(b):
         for k in range(4):
             lo = 768 * k
             dh = dot_nn(cot[tok(b), :], W[:, lo : lo + 768])
             B[tok(b), lo : lo + 768] = (dh * B[tok(b), lo : lo + 768].astype(F32)).astype(BF)
+
+    def block_output(b):
         branch = dot_nt(A[tok(b), :], W[...])
         E[tok(b), :] = (R[tok(b), :] + branch + vec[7:8, :]).astype(BF)
+        send_out(b)
+
+    def send_out(b):
         pl.when(swapped)(lambda: out_remote(b).start())
         pl.when(kept)(lambda: out_local(b).start())
 
-    def t_mlp0():
-        ld_wd.wait()
-        ld_gp.wait()
-        ld_res.wait()
-        blocks(mlp_back, 0, 2)
-
-    def t_mlp1():
-        blocks(mlp_back, 2, 4)
-        ld_wu.start()
-        ld_qkvm.start()
-        ld_n2.wait()
-
-    def t_up(v):
-        u = v - 6
-        ubs[0:1, wide(u)] = dot_nn(ones, B[:, wide(u)])[0:1, :]
-        gradient(n2[...], B[:, wide(u)], v % RING)
+    def loads(k):
+        if k == 0:
+            for p in range(2):
+                gather_drain(p)
+            ld_wu.start()
+            ld_qkvm.start()
+            return
+        ld_wa.start()
+        ld_xv.start()
+        for b in range(4):
+            pl.when(swapped)(lambda: out_remote(b).wait_send())
+            pl.when(kept)(lambda: out_local(b).wait())
+        ld_nrm.start()
+
+    def t_up(lo, n):
+        once(ld_n2)
+
+        def one(u):
+            ubs[pl.ds(u, 1), :] = dot_nn(ones, B[:, wide(u)])[0:1, :]
+            gradient(n2[...], B[:, wide(u)], u % RING)
+
+        span(one, lo, n)
+        if lo + n == 4:
+            vg[8:12, :] = ubs[0:4, :]
 
     def norm_back(dn, v, gain):
         hat, scale = norm_parts(v)
@@ -627,27 +715,13 @@
         vg[5:6, :] = vg[5:6, :] + dgain
         vg[6:7, :] = vg[6:7, :] + dshift
 
-    def t_norm2():
-        for k in range(4):
-            vg[8 + k : 9 + k, :] = ubs[0:1, D * k : D * k + D]
-        ld_wu.wait()
-        blocks(second_norm)
-        ld_wa.start()
-        ld_xv.start()
-        for b in range(4):
-            pl.when(swapped)(lambda: out_remote(b).wait_send())
-            pl.when(kept)(lambda: out_local(b).wait())
-        ld_nrm.start()
+    def t_out(k):
+        once(ld_qkvm)
+        vg[4:5, :] = dot_nn(ones, B[:, 3 * D :])[0:1, :]
+        gradient(A[:, 3 * D :], B[:, 3 * D :], 8 % RING)
 
     def mixed_back(b):
         A[tok(b), 3 * D :] = dot_nt(B[tok(b), 3 * D :], W[:, 3 * D :]).astype(BF)
-
-    def t_out():
-        ld_qkvm.wait()
-        vg[4:5, :] = dot_nn(ones, B[:, 3 * D :])[0:1, :]
-        gradient(A[:, 3 * D :], B[:, 3 * D :], 8 % RING)
-        ld_wa.wait()
-        blocks(mixed_back)
 
     def attention_back(i):
         low, high = head_masks()
@@ -674,26 +748,38 @@
             both = dot_tn(ds, q) * SCALE
             B[r, D + col : D + col + 128] = jnp.where(lane, both[:128], both[128:]).astype(BF)
 
-    def t_att(v):
-        lo = (v - 12) * 4
-        blocks(lambda i: attention_back(lo + i))
-
-    def t_qkv(v):
-        u = v - 14
-
-        @pl.when(u == 0)
-        def _():
-            ld_nrm.wait()
+    def t_att(lo, n):
+        span(attention_back, 2 * lo, 2 * n)
+
+    def t_qkv(lo, n):
+        once(ld_nrm)
+        if lo == 0:
             vg[2:3, :] = dot_nn(ones, B[:, 0:D])[0:1, :]
             vg[3:4, :] = dot_nn(ones, B[:, 2 * D : 3 * D])[0:1, :]
-
-        gradient(E[...], B[:, wide(u)], (v - 5) % RING)
+        span(lambda u: gradient(E[...], B[:, wide(u)], (u + 1) % RING), lo, n)
 
     def ig_remote(b):
-        return remote(R.at[tok(b)], ig_o.at[tok(b)], igs.at[b], igr.at[b], partner)
+        return remote(n2.at[tok(b)], ig_land.at[tok(b)], igs.at[b], igr.at[b], partner)
 
     def ig_local(b):
         return pltpu.make_async_copy(R.at[tok(b)], ig_o.at[tok(b)], igr.at[b])
+
+    ld_land = load(ig_land, cot, 15)
+    ld_ig = pltpu.make_async_copy(R, ig_o, lsem.at[16])
+
+    def land(k):
+        @pl.when(swapped)
+        def _():
+            for b in range(4):
+                ig_remote(b).wait_recv()
+            ld_land.start()
+            ld_land.wait()
+
+            def one(b):
+                R[tok(b), :] = cot[tok(b), :].astype(F32)
+
+            span(one, 0, 4)
+            ld_ig.start()
 
     def first_norm_back(b):
         dn = dot_nt(B[tok(b), : 3 * D], W[:, : 3 * D])
@@ -701,7 +787,14 @@
         R[tok(b), :] = R[tok(b), :] + d
         vg[0:1, :] = vg[0:1, :] + dgain
         vg[1:2, :] = vg[1:2, :] + dshift
-        pl.when(swapped)(lambda: ig_remote(b).start())
+        send_ig(b)
+
+    def send_ig(b):
+        @pl.when(swapped)
+        def _():
+            n2[tok(b), :] = R[tok(b), :].astype(BF)
+            ig_remote(b).start()
+
         pl.when(kept)(lambda: ig_local(b).start())
 
     def cp_slice(j):
@@ -714,9 +807,7 @@
 
         lax.fori_loop(0, 8, step, 0)
 
-    def t_norm1():
-        ld_xv.wait()
-        blocks(first_norm_back)
+    def send_slices(k):
         for j in range(8):
             vsl[j, :, 0:SHARD] = vg[:, SHARD * j : SHARD * j + SHARD]
 
@@ -729,7 +820,7 @@
     def cp_change(k):
         return remote(vdl.at[g], vdl.at[g], vds.at[k], vdr.at[g], members[k])
 
-    def t_vec_adam():
+    def t_vec_adam(k):
         def step(s, carry):
             pl.when(jnp.logical_or(swapped, s != 2 * z + c))(
                 lambda: remote(vrc.at[s], vrc.at[s], vss.at[0], vsr.at[s], partner).wait_recv()
@@ -738,14 +829,16 @@
 
         lax.fori_loop(0, 8, step, 0)
         grad = jnp.sum(vrc[...], axis=0)[0:12, 0:SHARD]
-        mom, sq, delta = adam_parts(v1[...], v2[...], vw[...], grad, RATE_VECTOR, 0.0)
+        first = jnp.concatenate([v1[r] for r in range(12)], axis=0)
+        second = jnp.concatenate([v2[r] for r in range(12)], axis=0)
+        mom, sq, delta = adam_parts(first, second, vw[...], grad, RATE_VECTOR, 0.0)
         vm_o[...] = mom
         vs_o[...] = sq
         vdl[g, 0:12, 0:SHARD] = delta
         for k in range(3):
             cp_change(k).start()
 
-    def t_vec_outer():
+    def t_vec_outer(k):
         for k in range(3):
             remote(vdl.at[froms[k]], vdl.at[froms[k]], vds.at[k], vdr.at[froms[k]], members[k]).wait_recv()
         mean = jnp.sum(vdl[...], axis=0)[0:12, 0:SHARD] * 0.25
@@ -756,28 +849,6 @@
     members = [dev(x, 1 - c, z, y), dev(1 - x, c, z, y), dev(1 - x, 1 - c, z, y)]
     froms = [2 * x + 1 - c, 2 * (1 - x) + c, 2 * (1 - x) + 1 - c]
 
-    def tasks(v):
-        pl.when(v < 4)(lambda: t_down(v))
-        pl.when(v == 4)(t_mlp0)
-        pl.when(v == 5)(t_mlp1)
-        pl.when(jnp.logical_and(v >= 6, v <= 9))(lambda: t_up(v))
-        pl.when(v == 10)(t_norm2)
-        pl.when(v == 11)(t_out)
-        pl.when(jnp.logical_and(v >= 12, v <= 13))(lambda: t_att(v))
-        pl.when(jnp.logical_and(v >= 14, v <= 16))(lambda: t_qkv(v))
-        pl.when(v == 17)(t_norm1)
-        pl.when(v == 19)(t_vec_adam)
-        pl.when(v == 21)(t_vec_outer)
-
-    def piece(v):
-        first = jnp.logical_and(v >= 0, v < 4)
-        second = jnp.logical_and(v >= 6, v < 10)
-        third = v == 11
-        fourth = jnp.logical_and(v >= 14, v < 17)
-        real = jnp.logical_or(jnp.logical_or(first, second), jnp.logical_or(third, fourth))
-        p = jnp.where(v < 4, v, jnp.where(v < 10, v - 2, jnp.where(v < 12, 8, v - 5)))
-        return real, p
-
     def cp_core(p):
         return remote(G.at[p % RING, 1 - c], S.at[p], d2s.at[p], d2r.at[p], dev(x, 1 - c, z, y))
 
@@ -799,8 +870,11 @@
 
     def s1(p):
         cp_core(p).wait_recv()
-        for t in range(4):
+
+        def one(t):
             S[p, t] = (S[p, t].astype(F32) + G[p % RING, c, t].astype(F32)).astype(BF)
+
+        span(one, 0, 4)
 
         @pl.when(z == 0)
         def _():
@@ -842,37 +916,22 @@
         return remote(S.at[p, z], FIN.at[p], fs.at[p], fr.at[p], partner)
 
     def col(p):
-        return pl.ds(pl.multiple_of(768 * jnp.where(p < 8, p % 4, (p + 3) % 4), 128), 768)
+        return pl.ds(768 * (p % 4 if p < 8 else (p + 3) % 4), 768)
 
     def state_loads(p, fn):
         q = p % 2
-
-        @pl.when(p < 8)
-        def _():
-            m = 1 - p // 4
-            for k, src in enumerate((m1, m2, mw, mo)):
-                fn(pltpu.make_async_copy(src.at[m, :, col(p)], IN.at[q, k], isem.at[q, k]))
-
-        @pl.when(p >= 8)
-        def _():
-            for k, src in enumerate((a1, a2, aw, ao)):
-                fn(pltpu.make_async_copy(src.at[:, col(p)], IN.at[q, k], isem.at[q, k]))
+        m = 1 - p // 4
+        for k, src in enumerate((m1, m2, mw, mo) if p < 8 else (a1, a2, aw, ao)):
+            src = src.at[m, :, col(p)] if p < 8 else src.at[:, col(p)]
+            fn(pltpu.make_async_copy(src, IN.at[q, k], isem.at[q, k]))
 
     def state_stores(p, ks, fn):
         q = p % 2
-
-        @pl.when(p < 8)
-        def _():
-            m = 1 - p // 4
-            for k in ks:
-                dst = (mm_o, ms_o, mp_o, mq_o)[k]
-                fn(pltpu.make_async_copy(OUT.at[q, k], dst.at[m, :, col(p)], osem.at[q, k]))
-
-        @pl.when(p >= 8)
-        def _():
-            for k in ks:
-                dst = (am_o, as_o, ap_o, aq_o)[k]
-                fn(pltpu.make_async_copy(OUT.at[q, k], dst.at[:, col(p)], osem.at[q, k]))
+        m = 1 - p // 4
+        for k in ks:
+            dst = ((mm_o, ms_o, mp_o, mq_o) if p < 8 else (am_o, as_o, ap_o, aq_o))[k]
+            dst = dst.at[m, :, col(p)] if p < 8 else dst.at[:, col(p)]
+            fn(pltpu.make_async_copy(OUT.at[q, k], dst, osem.at[q, k]))
 
     def start(cp):
         cp.start()
@@ -881,7 +940,6 @@
         cp.wait()
 
     def s4(p):
-        state_loads(p, start)
         pl.when(z > 0)(lambda: add_in(p, z, 0))
         pl.when(z < 3)(lambda: add_in(p, z, 4))
 
@@ -894,12 +952,18 @@
             FIN[p] = S[p, z]
 
     def cp_delta(p, k):
-        return remote(DL.at[p, g], DL.at[p, g], ls.at[p, k], lr.at[p, g], members[k])
+        i = (g, g, froms[1])[k]
+        return remote(DL.at[p, i], DL.at[p, i], ls.at[p, k], lr.at[p, i], members[1 if k == 1 else 0])
+
+    def got_delta(p, k):
+        i = froms[k]
+        remote(DL.at[p, i], DL.at[p, i], ls.at[p, 0], lr.at[p, i], members[k]).wait_recv()
 
     def s5(p):
         pl.when(swapped)(lambda: cp_final(p).wait_recv())
         state_loads(p, wait)
-        pl.when(p >= 2)(lambda: state_stores(p - 2, (0, 1), wait))
+        if p >= 2:
+            state_stores(p - 2, (0, 1), wait)
         q = p % 2
 
         def rows(i, carry):
@@ -913,14 +977,19 @@
             return carry
 
         lax.fori_loop(0, 3, rows, 0)
-        for k in (1, 2, 0):
+        for k in (1, 0):
             cp_delta(p, k).start()
         state_stores(p, (0, 1), start)
 
     def s6(p):
-        for k in range(3):
-            remote(DL.at[p, froms[k]], DL.at[p, froms[k]], ls.at[p, k], lr.at[p, froms[k]], members[k]).wait_recv()
-        pl.when(p >= 2)(lambda: state_stores(p - 2, (2, 3), wait))
+        got_delta(p, 1)
+        cp_delta(p, 2).start()
+
+    def s7(p):
+        got_delta(p, 0)
+        got_delta(p, 2)
+        if p >= 2:
+            state_stores(p - 2, (2, 3), wait)
         q = p % 2
 
         def rows(i, carry):
@@ -937,34 +1006,25 @@
         lax.fori_loop(0, 3, rows, 0)
         state_stores(p, (2, 3), start)
 
-    def slot(v, carry):
-        tasks(v)
-        for k, fn in ((0, s0), (1, s1), (2, s2), (3, s3), (6, s6), (4, s4), (5, s5)):
-            real, p = piece(v - k)
-            pl.when(real)(functools.partial(fn, p))
-        return carry
-
-    lax.fori_loop(0, 23, slot, 0)
-
-    def drain(p, carry):
-        @pl.when(jnp.logical_or(z == 0, z == 3))
-        def _():
-            for k in range(3):
-                remote(S.at[p, k], ZI.at[p, k], zs.at[p, k], zr.at[p, k], partner).wait_send()
-
-        @pl.when(jnp.logical_and(z > 0, z < 3))
-        def _():
-            for k in range(3):
-                remote(S.at[p, k], ZI.at[p, k], zs.at[p, k], zr.at[p, k], partner).wait_send()
-
+    sums = (s0, s1, s2, s3, s4, s5, s6, s7)
+    does = {
+        "g": lambda p, s: stages[s](p), "r": lambda p, k: sums[k](p), "il": lambda p: state_loads(p, start),
+        "st": lambda k: None, "gd": t_down, "dh": spanned(hidden_back, ld_gp), "bo": spanned(block_output, ld_res),
+        "ld": loads, "gu": t_up, "n2": spanned(second_norm, ld_wu), "go": t_out, "dm": spanned(mixed_back, ld_wa),
+        "ab": t_att, "gq": t_qkv, "n1": spanned(first_norm_back, ld_xv), "ic": land,
+        "vs": send_slices, "va": t_vec_adam, "vo": t_vec_outer,
+    }
+    for name, *at in ORDER_BACKWARD:
+        does[name](*at)
+
+    for p in range(RS):
+        for k in range(3):
+            remote(S.at[p, k], ZI.at[p, k], zs.at[p, k], zr.at[p, k], partner).wait_send()
         pl.when(swapped)(lambda: cp_final(p).wait_send())
         for k in range(3):
             cp_delta(p, k).wait_send()
-        return carry
-
-    lax.fori_loop(0, RS, drain, 0)
     for p in (RS - 2, RS - 1):
-        state_stores(jnp.int32(p), (0, 1, 2, 3), wait)
+        state_stores(p, (0, 1, 2, 3), wait)
     each_slice(lambda j: cp_slice(j).wait_send())
     for k in range(3):
         cp_change(k).wait_send()
@@ -973,14 +1033,16 @@
         @pl.when(swapped)
         def _():
             out_remote(b).wait_recv()
-            ig_remote(b).wait()
+            ig_remote(b).wait_send()
 
         @pl.when(kept)
         def _():
             ig_local(b).wait()
 
-
-def backward(fwd, states):
+    pl.when(swapped)(lambda: ld_ig.wait())
+
+
+def backward(cot, fwd, states):
     any_ = pl.BlockSpec(memory_space=pl.ANY)
     vm = pl.BlockSpec(memory_space=pltpu.VMEM)
     dma = pltpu.SemaphoreType.DMA
@@ -992,9 +1054,10 @@
         out_shape=(
             jax.ShapeDtypeStruct((T, D), BF), jax.ShapeDtypeStruct((T, D), F32),
             attn, attn, attn, attn, mlp, mlp, mlp, mlp, vect, vect, vect, vect,
+            jax.ShapeDtypeStruct((T, D), BF),
         ),
-        in_specs=[any_] * 9 + [vm, vm] + [any_] * 8 + [vm] * 4,
-        out_specs=(any_,) * 10 + (vm,) * 4,
+        in_specs=[any_] * 10 + [vm, vm] + [any_] * 8 + [vm] * 4,
+        out_specs=(any_,) * 10 + (vm,) * 4 + (any_,),
         scratch_shapes=[
             pltpu.VMEM((T, FF), BF), pltpu.VMEM((T, FF), BF), pltpu.VMEM((D, FF), BF),
             pltpu.VMEM((T, D), BF), pltpu.VMEM((T, D), BF), pltpu.VMEM((T, D), BF), pltpu.VMEM((T, D), F32),
@@ -1002,15 +1065,16 @@
             pltpu.VMEM((RS, 5, SHARD, 768), BF), pltpu.VMEM((RS, SHARD, 768), BF),
             pltpu.VMEM((RS, 4, SHARD, 768), BF),
             pltpu.VMEM((2, 4, SHARD, 768), F32), pltpu.VMEM((2, 4, SHARD, 768), F32),
-            pltpu.VMEM((16, D), F32), pltpu.VMEM((1, FF), F32),
+            pltpu.VMEM((16, D), F32), pltpu.VMEM((8, D), F32),
             pltpu.VMEM((8, 16, 128), F32), pltpu.VMEM((8, 16, 128), F32), pltpu.VMEM((4, 16, 128), F32),
-            dma((11,)), dma((RS,)), dma((RS,)), dma((RS, 3)), dma((RS, 5)), dma((RS,)), dma((RS,)),
+            dma((17,)), dma((RS,)), dma((RS,)), dma((RS, 3)), dma((RS, 5)), dma((RS,)), dma((RS,)),
             dma((RS, 3)), dma((RS, 4)), dma((2, 4)), dma((2, 4)), dma((4,)), dma((4,)), dma((4,)), dma((4,)),
             dma((8,)), dma((8,)), dma((3,)), dma((4,)),
+            *GATHER_SEMS(2),
         ],
         compiler_params=pltpu.CompilerParams(collective_id=2, has_side_effects=True, vmem_limit_bytes=63 * 2**20),
         name="backward",
-    )(*fwd, *states)
+    )(cot, *fwd, *states)
 
 
 def fast(
@@ -1019,18 +1083,18 @@
     mlp_weight, mlp_first, mlp_second, mlp_outer,
     vector_weight, vector_first, vector_second, vector_outer,
 ):
-    seg = segments[0].reshape(8, 128) + 8 * (lax.broadcasted_iota(jnp.int32, (8, 128), 1) // SEQ)
-    fwd = forward(inputs[0], cotangent[0], seg, attn_weight, mlp_weight, vector_weight)
+    fwd = forward(inputs[0], cotangent[0], segments[0], attn_weight, mlp_weight, vector_weight)
     out = backward(
+        cotangent[0],
         fwd,
         (
             attn_weight, attn_first[0], attn_second[0], attn_outer,
             mlp_weight, mlp_first[0], mlp_second[0], mlp_outer,
-            vector_weight, vector_first[0], vector_second[0], vector_outer,
+            vector_weight, jnp.transpose(vector_first, (1, 0, 2)), jnp.transpose(vector_second, (1, 0, 2)), vector_outer,
         ),
     )
-    lead = (1, 1, 1, 1, 0, 0, 1, 1, 0, 0, 1, 1, 0, 0)
-    return tuple(v[None] if k else v for v, k in zip(out, lead))
+    lead = (1, 1, 1, 1, 0, 0, 1, 1, 0, 0, 0, 0, 0, 0)
+    return tuple(v[None] if k else v for v, k in zip(finish(out[:14]), lead))
 
 
 def norm_apply(values, gain, shift):

time: 337 us -> 262 us (0.78)
  Pallas kernels: 308 us -> 257 us
  local copies, waits for them, and re-layouts: 26.9 us -> 0 us
    pallas_call x1, Pallas kernels: 199 us -> 167 us  [backward(): pl.pallas_call(backward_kernel, out_shape=(jax.ShapeDtypeStruct((T, D), B...]
    unnamed x37 -> x0, local copies, waits for them, and re-layouts: 26.1 us -> none
    pallas_call x1 -> x2, Pallas kernels: 109 us -> 89.7 us  [the longest x1 74.5 us: forward(): pl.pallas_call(forward_kernel, out_shape=(jax.ShapeDtypeStruct((2, D, FF)...]
where the time goes in v3:
time: 262 us; the launch traced here: 258 us
  Pallas kernels  257 us (98%)
    pallas_call x1, Pallas kernels, backward(): pl.pallas_call(backward_kernel, out_shape=(jax.ShapeDtypeStruct((T, D), B...  167 us
    pallas_call x1, Pallas kernels, forward(): pl.pallas_call(forward_kernel, out_shape=(jax.ShapeDtypeStruct((2, D, FF)...  74.5 us
    pallas_call x1, Pallas kernels, finish(): pl.pallas_call(final_kernel, out_shape=(*shapes, thin, thin, *[jax.ShapeD...  15.3 us

profile of v3, /device:TPU:0, one launch (start us, length us, event | category | flops | bytes accessed | tf_op | source)
XLA Modules:
  0.0 257.7 jit_solution(4057939331773211109)
XLA Ops:
  0.6 74.5 %forward.1 = (bf16[2,768,3072]{2,1,0:T(8,128)(2,1)}, bf16[1024,3072]{1,0:T(8,128)(2,1)}, bf16[1024,3072]{1,0:T(8,128)(2,1)}, bf16[1024,3072]{1,0:T(8,128)(2,1)},...) custom-call(bf16[1024,768]{1,0:T(8,128)(2,1)} %bitcast.21, ...), custom_call_target="tpu_custom_call" | custom-call | tf_op jit(solution)/shard_map/forward/pallas_call | solution.py:482
  75.1 167.1 %backward.1 = (bf16[1024,768]{1,0:T(8,128)(2,1)}, f32[1024,768]{1,0:T(8,128)}, f32[96,3072]{1,0:T(8,128)}, f32[96,3072]{1,0:T(8,128)}, f32[96,3072]{1,0:T(8,128)...) custom-call(bf16[1024,768]{1,0:T(8,128)(2,1)} %bitcast.18, ...), custom_call_target="tpu_custom_call" | custom-call | tf_op jit(solution)/shard_map/backward/pallas_call | solution.py:1052
  242.2 15.3 %finish.1 = (bf16[1024,768]{1,0:T(8,128)(2,1)}, f32[1024,768]{1,0:T(8,128)}, f32[96,3072]{1,0:T(8,128)}, f32[96,3072]{1,0:T(8,128)}, f32[96,3072]{1,0:T(8,128)},...) custom-call(bf16[1024,768]{1,0:T(8,128)(2,1)} %get-tuple-element.64., ...), custom_call_target="tpu_custom_call" | custom-call | tf_op jit(solution)/shard_map/finish/pallas_call | solution.py:531
